TPU v7x, 512 devices: a whole 4x8x8 slice. The times are simulated.
512 devices in a mesh: row: 16 (over z, core), col: 4 (over y_hi), rep: 8 (over y_lo, x).
Axes of the slice: x: 4, y: 8 (y_hi: 4, y_lo: 2; y = y_hi * 2 + y_lo), z: 8, core: 2. Of those that a mesh axis runs over, the one named last changes fastest.
Arguments:
- features: bfloat16 [65536, 128], P(('row', 'col', 'rep')), may hold values from -6 to 6
- weight_in: bfloat16 [128, 128], replicated, may hold values from -0.5 to 0.5
- weight_hidden: bfloat16 [128, 128], replicated, may hold values from -0.5 to 0.5
- tile_rows: int32 [16, 32, 96], P('row', ('col', 'rep')), may hold values from 0 to 31
- tile_cols: int32 [16, 32, 96], P('row', ('col', 'rep')), may hold values from 0 to 15
- tile_values: bfloat16 [16, 32, 96, 128, 128], P('row', ('col', 'rep')), may hold values from -0.5 to 0.5
- tile_counts: int32 [16, 32], P('row', ('col', 'rep')), may hold values from 48 to 96, as said below
- cotangent: bfloat16 [65536, 128], P(('row', 'col', 'rep')), may hold values from -0.0234375 to 0.0234375
Outputs:
- logits: float32 [65536, 128], P(('row', 'col', 'rep'))
- grad_weight_in: float32 [128, 128], replicated
- grad_weight_hidden: float32 [128, 128], replicated
Inputs may be any that keep to these rules, and one draw needn't show every extreme that they name: `tile_rows`: only an owner's live slots count; the data in the other slots is arbitrary. Two live slots may name the same tile row and column; their tiles add. `tile_counts`: in every draw some owner has all 96 slots live.
All inputs are finite; a program needn't handle non-finite values.
Results may differ from a plain program's by a relative error of at most 0.04.
Values may be sent and summed in bfloat16 or wider, within the bound.
A program may use at most 64 MiB of HBM per device.

v0:
```python
import jax
import jax.numpy as jnp
from jax import lax
from jax.sharding import PartitionSpec as P


def spread_tiles(tile_block, row_index, col_index, tile_count, source, out_blocks, backward):
    slot_total = tile_block.shape[0]
    group_size = min(16, slot_total)
    tile_size = tile_block.shape[1]
    feature_width = source.shape[2]

    def one_group(turn_index, running):
        first_slot = turn_index * group_size
        block_part = lax.dynamic_slice_in_dim(tile_block, first_slot, group_size, 0)
        row_part = lax.dynamic_slice_in_dim(row_index, first_slot, group_size, 0)
        col_part = lax.dynamic_slice_in_dim(col_index, first_slot, group_size, 0)
        live_mask = (first_slot + jnp.arange(group_size, dtype=jnp.int32) < tile_count).astype(
            jnp.float32
        )
        if backward:
            picked = source[row_part]
            products = jnp.einsum(
                "tji,tjh->tih", block_part, picked, preferred_element_type=jnp.float32
            )
            target = col_part
        else:
            picked = source[col_part]
            products = jnp.einsum(
                "tij,tjh->tih", block_part, picked, preferred_element_type=jnp.float32
            )
            target = row_part
        return running.at[target].add(products * live_mask[:, None, None])

    turns = (tile_count + group_size - 1) // group_size
    start_sum = jnp.zeros((out_blocks, tile_size, feature_width), jnp.float32)
    return lax.fori_loop(0, turns, one_group, start_sum)


def body(
    features, weight_in, weight_hidden, tile_rows, tile_cols, tile_values, tile_counts, cotangent
):
    own_rows = features.shape[0]
    tile_block = tile_values[0, 0]
    row_index = tile_rows[0, 0]
    col_index = tile_cols[0, 0]
    tile_count = tile_counts[0, 0]
    tile_size = tile_block.shape[1]
    feature_width = weight_hidden.shape[1]
    range_blocks = lax.axis_size(("col", "rep")) * own_rows // tile_size

    def forward_layer(inputs, weight):
        own_products = jnp.dot(inputs, weight, preferred_element_type=jnp.float32).astype(
            jnp.bfloat16
        )
        column = lax.all_gather(own_products, "row", axis=0, tiled=True)
        column_blocks = column.reshape(column.shape[0] // tile_size, tile_size, feature_width)
        partial_value = spread_tiles(
            tile_block, row_index, col_index, tile_count, column_blocks, range_blocks, False
        )
        partial_rows = partial_value.reshape(range_blocks * tile_size, feature_width)
        return lax.psum_scatter(
            partial_rows.astype(jnp.bfloat16), ("col", "rep"), scatter_dimension=0, tiled=True
        ).astype(jnp.float32)

    def backward_layer(grad_own):
        gathered = lax.all_gather(grad_own, ("col", "rep"), axis=0, tiled=True)
        range_source = gathered.reshape(range_blocks, tile_size, feature_width)
        list_blocks = lax.axis_size("row") * own_rows // tile_size
        partial_value = spread_tiles(
            tile_block, row_index, col_index, tile_count, range_source, list_blocks, True
        )
        partial_rows = partial_value.reshape(list_blocks * tile_size, feature_width)
        return lax.psum_scatter(
            partial_rows.astype(jnp.bfloat16), "row", scatter_dimension=0, tiled=True
        )

    contract_rows = (((0,), (0,)), ((), ()))
    contract_cols = (((1,), (1,)), ((), ()))
    sum_first = forward_layer(features, weight_in)
    hidden = jax.nn.silu(sum_first).astype(jnp.bfloat16)
    logits = forward_layer(hidden, weight_hidden)
    grad_products_second = backward_layer(cotangent)
    term_second = lax.dot_general(
        hidden, grad_products_second, contract_rows, preferred_element_type=jnp.float32
    )
    grad_hidden = lax.dot_general(
        grad_products_second, weight_hidden, contract_cols, preferred_element_type=jnp.float32
    )
    gate_value = jax.nn.sigmoid(sum_first)
    grad_sum_first = (grad_hidden * gate_value * (1.0 + sum_first * (1.0 - gate_value))).astype(
        jnp.bfloat16
    )
    grad_products_first = backward_layer(grad_sum_first)
    term_first = lax.dot_general(
        features, grad_products_first, contract_rows, preferred_element_type=jnp.float32
    )
    grad_weight_in, grad_weight_hidden = lax.psum((term_first, term_second), ("row", "col", "rep"))
    return (logits, grad_weight_in, grad_weight_hidden)


def solution(mesh):
    return jax.shard_map(
        body,
        mesh=mesh,
        in_specs=(
            P(("row", "col", "rep"), None),
            P(),
            P(),
            P("row", ("col", "rep"), None),
            P("row", ("col", "rep"), None),
            P("row", ("col", "rep"), None, None, None),
            P("row", ("col", "rep")),
            P(("row", "col", "rep"), None),
        ),
        out_specs=(P(("row", "col", "rep"), None), P(), P()),
        check_vma=False,
    )
```

profile of v0, /device:TPU:1, one launch (start us, length us, event | category | flops | bytes accessed | tf_op | source)
XLA Modules:
  0.0 1056.3 jit_solution(13898889091900058484)
XLA Ops:
  9.5 25.9 %all_gather.12 = bf16[2048,128]{1,0:T(8,128)(2,1)S(1)} all-gather(bf16[128,128]{1,0:T(8,128)(2,1)S(1)} %convolution_convert_fusion.1), channel_id=1, replica_groups=mesh['row'=16,'col'=4,'rep'=8] {'row'}, dimensions={0}, use_global_device_ids=true | all-gather | bytes 557056 | tf_op jit(solution)/shard_map/all_gather | solution.py:56
  37.1 30.5 %while.40 = (s32[]{:T(128)}, f32[32,128,128]{2,1,0:T(8,128)}, s32[]{:T(128)}, s32[96]{0:T(128)S(1)}, bf16[96,128,128]{2,1,0:T(8,128)(2,1)}, /*index=5*/s32[96]{0...) while((s32[]{:T(128)}, f32[32,128,128]{2,1,0:T(8,128)}, ...), condition=%wide.region_2.3_spmd, body=%wide.region_0.2_spmd.sunk | while | flops 67634328 | bytes 6296307 | solution.py:37
  39.8 3.3 scatter_fusion
  45.9 3.4 scatter_fusion
  52.0 3.4 scatter_fusion
  58.1 3.4 scatter_fusion
  64.2 3.4 scatter_fusion
  67.5 2.9 convert_element_type.71
  70.5 2.8 copy.11
  73.3 20.5 %all-gather.3.cloned.1.call-done = bf16[4096,128]{1,0:T(8,128)(2,1)} async-done(((bf16[128,128]{1,0:T(8,128)(2,1)}), bf16[4096,128]{1,0:T(8,128)(2,1)}) %all-gather.3.cloned.1.call-update) | async-done | bytes 1048592 | tf_op jit(solution)/shard_map/all_gather | solution.py:67
  93.9 28.1 %while.42 = (s32[]{:T(128)}, f32[16,128,128]{2,1,0:T(8,128)S(1)}, s32[]{:T(128)}, s32[96]{0:T(128)S(1)}, bf16[96,128,128]{1,2,0:T(8,128)(2,1)}, /*index=5*/s32[9...) while((s32[]{:T(128)}, f32[16,128,128]{2,1,0:T(8,128)S(1)}, ...), condition=%wide.region_10.11_spmd, body=%wide.region_8.10_spmd.sunk | while | flops 67634328 | bytes 6296307 | solution.py:37
  94.0 1.9 gather_fusion.2
  99.6 1.9 gather_fusion.2
  105.2 1.9 gather_fusion.2
  116.4 1.9 gather_fusion.2
  122.9 192.0 %reduce-scatter.5.cloned.1.call-done = bf16[128,128]{1,0:T(8,128)(2,1)} async-done(((bf16[4096,128]{1,0:T(8,128)(2,1)}), bf16[128,128]{1,0:T(8,128)(2,1)}) %reduce-scatter.5.cloned.1.call-update) | async-done | bytes 32784 | tf_op jit(solution)/shard_map/reduce_scatter | solution.py:62
  315.0 63.7 %reduce-scatter.9.cloned.1.call-done = bf16[128,128]{1,0:T(8,128)(2,1)} async-done(((bf16[2048,128]{1,0:T(8,128)(2,1)}), bf16[128,128]{1,0:T(8,128)(2,1)}) %reduce-scatter.9.cloned.1.call-update) | async-done | bytes 32784 | tf_op jit(solution)/shard_map/reduce_scatter | solution.py:74
  381.2 19.1 %all_gather.13 = bf16[2048,128]{1,0:T(8,128)(2,1)S(1)} all-gather(bf16[128,128]{1,0:T(8,128)(2,1)S(1)} %convolution_convert_fusion), channel_id=1, replica_groups=mesh['row'=16,'col'=4,'rep'=8] {'row'}, dimensions={0}, use_global_device_ids=true | all-gather | bytes 557056 | tf_op jit(solution)/shard_map/all_gather | solution.py:56
  400.3 60.2 %all-gather.5.cloned.1.call-done = bf16[4096,128]{1,0:T(8,128)(2,1)} async-done(((bf16[128,128]{1,0:T(8,128)(2,1)}), bf16[4096,128]{1,0:T(8,128)(2,1)}) %all-gather.5.cloned.1.call-update) | async-done | bytes 1048592 | tf_op jit(solution)/shard_map/all_gather | solution.py:67
  460.6 28.1 %while.43 = (s32[]{:T(128)}, f32[16,128,128]{2,1,0:T(8,128)S(1)}, s32[]{:T(128)}, s32[96]{0:T(128)S(1)}, bf16[96,128,128]{1,2,0:T(8,128)(2,1)}, /*index=5*/s32[9...) while((s32[]{:T(128)}, f32[16,128,128]{2,1,0:T(8,128)S(1)}, ...), condition=%wide.region_14.15_spmd, body=%wide.region_12.14_spmd.sunk | while | flops 67634328 | bytes 6296307 | solution.py:37
  460.7 1.9 gather_fusion.3
  472.0 1.9 gather_fusion.3
  491.2 30.5 %while.41 = (s32[]{:T(128)}, f32[32,128,128]{2,1,0:T(8,128)}, s32[]{:T(128)}, s32[96]{0:T(128)S(1)}, bf16[96,128,128]{2,1,0:T(8,128)(2,1)}, /*index=5*/s32[96]{0...) while((s32[]{:T(128)}, f32[32,128,128]{2,1,0:T(8,128)}, ...), condition=%wide.region_6.7_spmd, body=%wide.region_4.6_spmd.sunk | while | flops 67634328 | bytes 6296307 | solution.py:37
  494.0 3.3 scatter_fusion.1
  500.1 3.4 scatter_fusion.1
  506.2 3.4 scatter_fusion.1
  512.3 3.4 scatter_fusion.1
  518.4 3.4 scatter_fusion.1
  521.7 2.8 convert_element_type.76
  525.4 29.5 %reduce-scatter.11.cloned.1.call-done = bf16[128,128]{1,0:T(8,128)(2,1)} async-done(((bf16[2048,128]{1,0:T(8,128)(2,1)}), bf16[128,128]{1,0:T(8,128)(2,1)}) %reduce-scatter.11.cloned.1.call-update) | async-done | bytes 32784 | tf_op jit(solution)/shard_map/reduce_scatter | solution.py:74
  556.5 217.5 %reduce-scatter.7.cloned.1.call-done = bf16[128,128]{1,0:T(8,128)(2,1)} async-done(((bf16[4096,128]{1,0:T(8,128)(2,1)}), bf16[128,128]{1,0:T(8,128)(2,1)}) %reduce-scatter.7.cloned.1.call-update) | async-done | bytes 32784 | tf_op jit(solution)/shard_map/reduce_scatter | solution.py:62
  775.5 271.0 %all-reduce.3.cloned.1.call-done = (f32[128,128]{0,1:T(8,128)}, f32[128,128]{1,0:T(8,128)}) async-done(((f32[128,128]{0,1:T(8,128)}, f32[128,128]{1,0:T(8,128)}), (f32[128,128]{0,1:T(8,128)}, f32[128,128]{1,0:T(8,128)})) %all-reduce.3.cloned.1.call-update) | async-done | bytes 131088 | tf_op jit(solution)/shard_map/psum | solution.py:98
  (146 shorter events, 87.9 us)
Async XLA Ops:
  7.2 371.5 %copy-start = (bf16[128,128]{1,0:T(8,128)(2,1)S(1)}, bf16[128,128]{1,0:T(8,128)(2,1)}, u32[]{:S(2)}) copy-start(bf16[128,128]{1,0:T(8,128)(2,1)} %param.18) | copy-start | bytes 98308
  7.2 29.9 %copy-start.2 = (s32[1,1,96]{2,1,0:T(1,128)S(1)}, s32[1,1,96]{2,1,0:T(1,128)}, u32[]{:S(2)}) copy-start(s32[1,1,96]{2,1,0:T(1,128)} %param.19) | copy-start | bytes 1156
  7.2 29.9 %copy-start.3 = (s32[1,1,96]{2,1,0:T(1,128)S(1)}, s32[1,1,96]{2,1,0:T(1,128)}, u32[]{:S(2)}) copy-start(s32[1,1,96]{2,1,0:T(1,128)} %param.20) | copy-start | bytes 1156
  7.2 86.6 %all-gather.3.cloned.1.call-start = ((), (), s32[]{:S(2)}) async-start(), calls=%async_computation.6 | async-start | bytes 1081344 | tf_op jit(solution)/shard_map/all_gather | solution.py:67
  7.9 307.0 %reduce-scatter.5.cloned.1.call-start = ((), (), s32[]{:S(2)}) async-start(), calls=%async_computation.4 | async-start | bytes 1081344 | tf_op jit(solution)/shard_map/reduce_scatter | solution.py:62
  67.5 3.0 copy-start.1
  70.4 308.3 %reduce-scatter.9.cloned.1.call-start = ((), (), s32[]{:S(2)}) async-start(), calls=%async_computation.7 | async-start | bytes 557056 | tf_op jit(solution)/shard_map/reduce_scatter | solution.py:74
  122.9 337.6 %all-gather.5.cloned.1.call-start = ((), (), s32[]{:S(2)}) async-start(), calls=%async_computation.8 | async-start | bytes 1081344 | tf_op jit(solution)/shard_map/all_gather | solution.py:67
  380.3 174.7 %reduce-scatter.11.cloned.1.call-start = ((), (), s32[]{:S(2)}) async-start(), calls=%async_computation.9 | async-start | bytes 557056 | tf_op jit(solution)/shard_map/reduce_scatter | solution.py:74
  489.6 284.5 %reduce-scatter.7.cloned.1.call-start = ((), (), s32[]{:S(2)}) async-start(), calls=%async_computation.5 | async-start | bytes 1081344 | tf_op jit(solution)/shard_map/reduce_scatter | solution.py:62
  521.7 2.8 copy-start.5
  521.7 2.8 copy-start.6
  521.7 33.2 %copy-start.4 = (bf16[128,128]{1,0:T(8,128)(2,1)S(1)}, bf16[128,128]{1,0:T(8,128)(2,1)}, u32[]{:S(2)}) copy-start(bf16[128,128]{1,0:T(8,128)(2,1)} %param.16) | copy-start | bytes 98308
  524.5 521.9 %all-reduce.3.cloned.1.call-start = ((), (), s32[]{:S(2)}) async-start(), calls=%async_computation.10 | async-start | bytes 262144 | tf_op jit(solution)/shard_map/psum | solution.py:98
Sparse Core Ops, SparseCore 0:
  11.2 82.5 all-gather.2
  98.2 216.7 reduce-scatter.4
  317.7 60.8 reduce-scatter.8
  382.8 77.7 all-gather.4
  489.7 65.1 reduce-scatter.10
  559.2 214.8 reduce-scatter.6
  779.9 266.5 all-reduce.2
where the time goes:
time: 1060 us
  waiting for transfers between devices  855 us (81%)
  other arithmetic  73.1 us (7%)
  blocking collectives  45 us (4%)
  local copies, waits for them, and re-layouts  34.4 us (3%)
  matrix products  32.5 us (3%)
  between operations  14.9 us (1%)
    reduce_scatter x2, waiting for transfers between devices, forward_layer(): lax.psum_scatter(partial_rows.astype(jnp.bfloat16), ('col', 'rep'), scatt...  410 us
    psum x1, waiting for transfers between devices, body(): lax.psum((term_first, term_second), ('row', 'col', 'rep'))  271 us
    reduce_scatter x2, waiting for transfers between devices, backward_layer(): lax.psum_scatter(partial_rows.astype(jnp.bfloat16), 'row', scatter_dimens...  93.3 us
    all_gather x2, waiting for transfers between devices, backward_layer(): gathered = lax.all_gather(grad_own, ('col', 'rep'), axis=0, tiled=True)  80.7 us
    scatter-add x20, other arithmetic, one_group(): return running.at[target].add(products * live_mask[:, None, None])  49.6 us
    all_gather x2, blocking collectives, forward_layer(): column = lax.all_gather(own_products, 'row', axis=0, tiled=True)  45 us
  transfers between devices with their start and end apart: 7, of which 7 were waited for; matrix products, arithmetic and copies ran while one was open for 10% of the time, Pallas kernels for 0%

commit v1 on v0

v1 whole, which is shorter than its diff:
```python
import functools

import jax
import jax.numpy as jnp
from jax import lax
from jax.experimental import pallas as pl
from jax.experimental.pallas import tpu as pltpu
from jax.sharding import PartitionSpec as P

MESH = pl.DeviceIdType.MESH
BF = jnp.bfloat16
F32 = jnp.float32
CONTRACT_LAST = (((1,), (1,)), ((), ()))


def ring_order(n):
    return sorted(range(1, n), key=lambda d: (min(d, n - d), d))


def kernel(
    nx, ny, nz, slots,
    meta, feat, w_in, w_hid, cot, tiles_hbm,
    logits, gw_in, gw_hid,
    tiles, col_src_0, col_src_1, row_src_0, row_src_1, part, send_f, rx_a, rx_b, mid_a, mid_b, ry_a, ry_b,
    send_b, r_core, mid_z, r_z, term, ar_row, ar_x, ar_y, ar_out,
    local_sem, ssem, rsem,
):
    row = lax.axis_index("row")
    col = lax.axis_index("col")
    rep = lax.axis_index("rep")
    reps_y = lax.axis_size("rep") // nx
    z, core = row // 2, row % 2
    y, x = col * reps_y + rep // nx, rep % nx

    def device(xx, yy, zz, cc):
        return (zz * 2 + cc, yy // reps_y, (yy % reps_y) * nx + xx)

    x_peers = [((x + d) % nx, device((x + d) % nx, y, z, core)) for d in ring_order(nx)]
    y_peers = [((y + d) % ny, device(x, (y + d) % ny, z, core)) for d in ring_order(ny)]
    z_peers = [((z + d) % nz, device(x, y, (z + d) % nz, core)) for d in ring_order(nz)]
    sibling = device(x, y, z, 1 - core)
    cross_peers = [((z + d) % nz, device(x, y, (z + d) % nz, 1 - core)) for d in ring_order(nz)]

    height = feat.shape[0]
    col_src, row_src = (col_src_0, col_src_1), (row_src_0, row_src_1)
    cut = 80

    tile_copy = pltpu.make_async_copy(tiles_hbm, tiles, local_sem.at[0])
    tile_copy.start()

    barrier = pltpu.get_barrier_semaphore()
    everyone = [p[1] for p in x_peers + y_peers + z_peers + cross_peers] + [sibling]
    for peer in everyone:
        pl.semaphore_signal(barrier, inc=1, device_id=peer, device_id_type=MESH)

    sends = []

    def push(phase, src, dst, peer):
        copy = pltpu.make_async_remote_copy(
            src_ref=src, dst_ref=dst, send_sem=ssem.at[phase], recv_sem=rsem.at[phase],
            device_id=peer, device_id_type=MESH,
        )
        copy.start()

    def landed(phase, ref):
        pltpu.make_async_copy(ref, ref, rsem.at[phase]).wait()

    def sent(phase, ref):
        sends.append((phase, ref))

    def gather_col_start(rnd, value):
        buf = col_src[rnd]
        buf[z, core] = value
        for _, peer in z_peers:
            push(rnd * 16 + 0, buf.at[z, core], buf.at[z, core], peer)
        sent(rnd * 16 + 0, buf.at[0 : nz - 1, 0])

    def gather_col_finish(rnd):
        buf = col_src[rnd]
        landed(rnd * 16 + 0, buf.at[0 : nz - 1, 0])
        push(rnd * 16 + 1, buf.at[:, core], buf.at[:, core], sibling)
        sent(rnd * 16 + 1, buf.at[:, 0])
        landed(rnd * 16 + 1, buf.at[:, 0])

    low, high = pl.ds(0, cut), pl.ds(cut, height - cut)

    def gather_row_start(rnd, value):
        buf = row_src[rnd]
        buf[y, x] = value
        for _, peer in y_peers:
            push(rnd * 16 + 2, buf.at[y, x, low], buf.at[y, x, low], peer)
        sent(rnd * 16 + 2, buf.at[0 : ny - 1, 0, low])
        for _, peer in x_peers:
            push(rnd * 16 + 3, buf.at[y, x, high], buf.at[y, x, high], peer)
        sent(rnd * 16 + 3, buf.at[0, 0 : nx - 1, high])

    def gather_row_second(rnd):
        buf = row_src[rnd]
        landed(rnd * 16 + 3, buf.at[0, 0 : nx - 1, high])
        for _, peer in y_peers:
            push(rnd * 16 + 5, buf.at[y, :, high], buf.at[y, :, high], peer)
        sent(rnd * 16 + 5, buf.at[0 : ny - 1, :, high])
        landed(rnd * 16 + 2, buf.at[0 : ny - 1, 0, low])
        for _, peer in x_peers:
            push(rnd * 16 + 4, buf.at[:, x, low], buf.at[:, x, low], peer)
        sent(rnd * 16 + 4, buf.at[:, 0 : nx - 1, low])

    def gather_row_finish(rnd):
        buf = row_src[rnd]
        landed(rnd * 16 + 5, buf.at[0 : ny - 1, :, high])
        landed(rnd * 16 + 4, buf.at[:, 0 : nx - 1, low])

    unroll = 8

    def spread_forward(rnd):
        src = col_src[rnd]

        def some(turn, acc):
            for i in range(unroll):
                k = turn * unroll + i
                c = meta[1, k]
                d = jnp.dot(tiles[meta[0, k]], src[c // 2, c % 2], preferred_element_type=F32)
                acc = jnp.where(meta[2, k] > 0, d, acc + d)
                part[k] = acc.astype(BF)
            return acc

        lax.fori_loop(0, slots // unroll, some, jnp.zeros((height, height), F32))

        def place(b, _):
            send_f[rnd, b // nx, b % nx] = part[meta[3, b]]
            return 0

        lax.fori_loop(0, nx * ny, place, 0)

    def spread_backward(rnd):
        src = row_src[rnd]

        def some(turn, acc):
            for i in range(unroll):
                k = turn * unroll + i
                r = meta[5, k]
                d = jnp.dot(src[r // nx, r % nx], tiles[meta[4, k]], preferred_element_type=F32)
                acc = jnp.where(meta[6, k] > 0, d, acc + d)
                part[k] = acc.astype(BF)
            return acc

        lax.fori_loop(0, slots // unroll, some, jnp.zeros((height, height), F32))

        def place(b, _):
            send_b[rnd, b // 2, b % 2] = part[meta[7, b]]
            return 0

        lax.fori_loop(0, nz * 2, place, 0)

    def reduce_rows_start(rnd):
        buf = send_f.at[rnd]
        for px, peer in x_peers:
            push(rnd * 16 + 6, buf.at[:, px, low], rx_a.at[rnd, x], peer)
        sent(rnd * 16 + 6, rx_a.at[rnd, 0 : nx - 1])
        for py, peer in y_peers:
            push(rnd * 16 + 7, buf.at[py, :, high], ry_b.at[rnd, y], peer)
        sent(rnd * 16 + 7, ry_b.at[rnd, 0 : ny - 1])

    def reduce_rows_second(rnd):
        buf = send_f.at[rnd]
        rx_a[rnd, x] = buf[:, x, 0:cut]
        ry_b[rnd, y] = buf[y, :, cut:height]
        landed(rnd * 16 + 6, rx_a.at[rnd, 0 : nx - 1])

        def add_x(b, _):
            total = rx_a[rnd, 0, b].astype(F32)
            for i in range(1, nx):
                total += rx_a[rnd, i, b].astype(F32)
            mid_a[rnd, b] = total.astype(BF)
            return 0

        lax.fori_loop(0, ny, add_x, 0)
        for py, peer in y_peers:
            push(rnd * 16 + 8, mid_a.at[rnd, py], ry_a.at[rnd, y], peer)
        sent(rnd * 16 + 8, ry_a.at[rnd, 0 : ny - 1])
        landed(rnd * 16 + 7, ry_b.at[rnd, 0 : ny - 1])

        def add_y(b, _):
            total = ry_b[rnd, 0, b].astype(F32)
            for i in range(1, ny):
                total += ry_b[rnd, i, b].astype(F32)
            mid_b[rnd, b] = total.astype(BF)
            return 0

        lax.fori_loop(0, nx, add_y, 0)
        for px, peer in x_peers:
            push(rnd * 16 + 9, mid_b.at[rnd, px], rx_b.at[rnd, x], peer)
        sent(rnd * 16 + 9, rx_b.at[rnd, 0 : nx - 1])
        ry_a[rnd, y] = mid_a[rnd, y]
        rx_b[rnd, x] = mid_b[rnd, x]

    def reduce_rows_finish(rnd):
        landed(rnd * 16 + 8, ry_a.at[rnd, 0 : ny - 1])
        top = ry_a[rnd, 0].astype(F32)
        for i in range(1, ny):
            top += ry_a[rnd, i].astype(F32)
        landed(rnd * 16 + 9, rx_b.at[rnd, 0 : nx - 1])
        bottom = rx_b[rnd, 0].astype(F32)
        for i in range(1, nx):
            bottom += rx_b[rnd, i].astype(F32)
        return jnp.concatenate([top, bottom], axis=0)

    def reduce_cols_start(rnd):
        buf = send_b.at[rnd]
        push(rnd * 16 + 10, buf.at[:, 1 - core], r_core.at[rnd], sibling)
        sent(rnd * 16 + 10, r_core.at[rnd])

    def reduce_cols_second(rnd):
        landed(rnd * 16 + 10, r_core.at[rnd])

        def add(b, _):
            mid_z[rnd, b] = (
                send_b[rnd, b, core].astype(F32) + r_core[rnd, b].astype(F32)
            ).astype(BF)
            return 0

        lax.fori_loop(0, nz, add, 0)
        for pz, peer in z_peers:
            push(rnd * 16 + 11, mid_z.at[rnd, pz], r_z.at[rnd, z], peer)
        sent(rnd * 16 + 11, r_z.at[rnd, 0 : nz - 1])
        r_z[rnd, z] = mid_z[rnd, z]

    def reduce_cols_finish(rnd):
        landed(rnd * 16 + 11, r_z.at[rnd, 0 : nz - 1])
        total = r_z[rnd, 0].astype(F32)
        for i in range(1, nz):
            total += r_z[rnd, i].astype(F32)
        return total.astype(BF)

    part[slots] = jnp.zeros((height, height), BF)
    products = jnp.dot(feat[...], w_in[...], preferred_element_type=F32).astype(BF)
    cot_t = cot[...].astype(F32).T.astype(BF)
    feat_t = feat[...].astype(F32).T.astype(BF)

    pl.semaphore_wait(barrier, len(everyone))

    gather_row_start(0, cot_t)
    gather_col_start(0, products)
    gather_row_second(0)
    gather_col_finish(0)
    tile_copy.wait()
    spread_forward(0)
    reduce_rows_start(0)
    gather_row_finish(0)
    spread_backward(0)
    reduce_cols_start(0)
    reduce_rows_second(0)
    reduce_cols_second(0)
    sum_first = reduce_rows_finish(0)
    gate = 1.0 / (1.0 + jnp.exp(-sum_first))
    hidden = (sum_first * gate).astype(BF)
    products = jnp.dot(hidden, w_hid[...], preferred_element_type=F32).astype(BF)
    gather_col_start(1, products)
    sum_t = sum_first.T
    gate_t = 1.0 / (1.0 + jnp.exp(-sum_t))
    hidden_t = (sum_t * gate_t).astype(BF)
    grad_t = reduce_cols_finish(0)
    grad_hidden_t = jnp.dot(w_hid[...], grad_t, preferred_element_type=F32)
    grad_sum_t = (grad_hidden_t * gate_t * (1.0 + sum_t * (1.0 - gate_t))).astype(BF)

    gather_row_start(1, grad_sum_t)
    term[1] = lax.dot_general(hidden_t, grad_t, CONTRACT_LAST, preferred_element_type=F32)
    gather_row_second(1)
    gather_col_finish(1)
    spread_forward(1)
    reduce_rows_start(1)
    gather_row_finish(1)
    spread_backward(1)
    reduce_cols_start(1)
    reduce_cols_second(1)
    reduce_rows_second(1)
    grad_first_t = reduce_cols_finish(1)
    term[0] = lax.dot_general(feat_t, grad_first_t, CONTRACT_LAST, preferred_element_type=F32)

    band = height // (2 * nz)
    row_peers = [(pz * 2 + core, peer) for pz, peer in z_peers]
    row_peers += [(pz * 2 + 1 - core, peer) for pz, peer in cross_peers]
    row_peers += [(z * 2 + 1 - core, sibling)]

    def rows_of(i):
        return pl.ds(pl.multiple_of(i * band, band), band)

    for i, peer in row_peers:
        push(12, term.at[:, rows_of(i)], ar_row.at[row], peer)
    sent(12, ar_row.at[0 : 2 * nz - 1])
    ar_row[row] = term[:, rows_of(row)]
    logits[...] = reduce_rows_finish(1)
    landed(12, ar_row.at[0 : 2 * nz - 1])
    total = ar_row[0]
    for i in range(1, 2 * nz):
        total += ar_row[i]
    ar_x[x] = total
    for _, peer in x_peers:
        push(13, ar_x.at[x], ar_x.at[x], peer)
    sent(13, ar_x.at[0 : nx - 1])
    landed(13, ar_x.at[0 : nx - 1])
    total = ar_x[0]
    for i in range(1, nx):
        total += ar_x[i]
    ar_y[y] = total
    for _, peer in y_peers:
        push(14, ar_y.at[y], ar_y.at[y], peer)
    sent(14, ar_y.at[0 : ny - 1])
    landed(14, ar_y.at[0 : ny - 1])
    total = ar_y[0]
    for i in range(1, ny):
        total += ar_y[i]
    ar_out[:, rows_of(row)] = total
    for _, peer in row_peers:
        push(15, ar_out.at[:, rows_of(row)], ar_out.at[:, rows_of(row)], peer)
    sent(15, ar_out.at[:, 0 : height - band])
    landed(15, ar_out.at[:, 0 : height - band])
    gw_in[...] = ar_out[0]
    gw_hid[...] = ar_out[1]

    for phase, ref in sends:
        pltpu.make_async_copy(ref, ref, ssem.at[phase]).wait()


def slot_order(group, other, count, groups, slots):
    at = jnp.arange(slots, dtype=jnp.int32)
    live = at < count
    key = jnp.where(live, group, groups)
    before = (key[None, :] < key[:, None]) | ((key[None, :] == key[:, None]) & (at[None, :] < at[:, None]))
    rank = jnp.sum(before, axis=1, dtype=jnp.int32)
    opens = jnp.logical_not(jnp.any((key[None, :] == key[:, None]) & (at[None, :] < at[:, None]), axis=1))
    here = rank[None, :] == at[:, None]
    values = jnp.stack([at, jnp.where(live, other, 0), opens.astype(jnp.int32)])
    placed = jnp.sum(jnp.where(here[None], values[:, None, :], 0), axis=2, dtype=jnp.int32)
    each = jnp.arange(groups, dtype=jnp.int32)
    upto = jnp.sum(key[None, :] <= each[:, None], axis=1, dtype=jnp.int32)
    found = jnp.any(key[None, :] == each[:, None], axis=1)
    last = jnp.where(found, upto - 1, slots)
    placed = jnp.pad(placed, ((0, 0), (0, 128 - slots)))
    return jnp.concatenate([placed, jnp.pad(last, (0, 128 - groups))[None]], axis=0)


def body(nx, features, weight_in, weight_hidden, tile_rows, tile_cols, tile_values, tile_counts, cotangent):
    nz = lax.axis_size("row") // 2
    ny = lax.axis_size(("col", "rep")) // nx
    slots, height = tile_values.shape[2], tile_values.shape[3]
    rows, cols, count = tile_rows[0, 0], tile_cols[0, 0], tile_counts[0, 0]
    meta = jnp.concatenate(
        [slot_order(rows, cols, count, nx * ny, slots), slot_order(cols, rows, count, nz * 2, slots)], axis=0
    )
    cut = 80
    rest = height - cut
    band = height // (2 * nz)
    block = (height, height)
    vmem = pl.BlockSpec(memory_space=pltpu.VMEM)
    return pl.pallas_call(
        functools.partial(kernel, nx, ny, nz, slots),
        out_shape=[jax.ShapeDtypeStruct(block, F32)] * 3,
        in_specs=[pl.BlockSpec(memory_space=pltpu.SMEM), vmem, vmem, vmem, vmem, pl.BlockSpec(memory_space=pl.ANY)],
        out_specs=[vmem] * 3,
        scratch_shapes=[
            pltpu.VMEM((slots,) + block, BF),
            pltpu.VMEM((nz, 2) + block, BF),
            pltpu.VMEM((nz, 2) + block, BF),
            pltpu.VMEM((ny, nx) + block, BF),
            pltpu.VMEM((ny, nx) + block, BF),
            pltpu.VMEM((slots + 1,) + block, BF),
            pltpu.VMEM((2, ny, nx) + block, BF),
            pltpu.VMEM((2, nx, ny, cut, height), BF),
            pltpu.VMEM((2, nx, rest, height), BF),
            pltpu.VMEM((2, ny, cut, height), BF),
            pltpu.VMEM((2, nx, rest, height), BF),
            pltpu.VMEM((2, ny, cut, height), BF),
            pltpu.VMEM((2, ny, nx, rest, height), BF),
            pltpu.VMEM((2, nz, 2) + block, BF),
            pltpu.VMEM((2, nz) + block, BF),
            pltpu.VMEM((2, nz) + block, BF),
            pltpu.VMEM((2, nz) + block, BF),
            pltpu.VMEM((2,) + block, F32),
            pltpu.VMEM((2 * nz, 2, band, height), F32),
            pltpu.VMEM((nx, 2, band, height), F32),
            pltpu.VMEM((ny, 2, band, height), F32),
            pltpu.VMEM((2,) + block, F32),
            pltpu.SemaphoreType.DMA((1,)),
            pltpu.SemaphoreType.DMA((32,)),
            pltpu.SemaphoreType.DMA((32,)),
        ],
        compiler_params=pltpu.CompilerParams(
            collective_id=0, has_side_effects=True, vmem_limit_bytes=48 * 1024 * 1024
        ),
    )(meta, features, weight_in, weight_hidden, cotangent, tile_values[0, 0])


def solution(mesh, nx=4):
    return jax.shard_map(
        functools.partial(body, nx),
        mesh=mesh,
        in_specs=(
            P(("row", "col", "rep"), None),
            P(),
            P(),
            P("row", ("col", "rep"), None),
            P("row", ("col", "rep"), None),
            P("row", ("col", "rep"), None, None, None),
            P("row", ("col", "rep")),
            P(("row", "col", "rep"), None),
        ),
        out_specs=(P(("row", "col", "rep"), None), P(), P()),
        check_vma=False,
    )
```

time: 1060 us -> 113 us (0.11)
  waiting for transfers between devices: 855 us -> 0 us
  Pallas kernels: 0 us -> 102 us
  other arithmetic: 73.1 us -> 2.88 us
  blocking collectives: 45 us -> 0 us
  matrix products: 32.5 us -> 0 us
  local copies, waits for them, and re-layouts: 34.4 us -> 6.82 us
  between operations: 14.9 us -> 1.4 us
    reduce_scatter x4 -> x0, waiting for transfers between devices: 503 us -> none  [the longest x2 410 us: forward_layer(): lax.psum_scatter(partial_rows.astype(jnp.bfloat16), ('col', 'rep'), scatt...]
    psum x1 -> x0, waiting for transfers between devices: 271 us -> none  [body(): lax.psum((term_first, term_second), ('row', 'col', 'rep'))]
    pallas_call x0 -> x1, Pallas kernels: none -> 102 us  [body(): pl.pallas_call(functools.partial(kernel, nx, ny, nz, slots), out_shape=[j...]
    all_gather x2 -> x0, waiting for transfers between devices: 80.7 us -> none  [backward_layer(): gathered = lax.all_gather(grad_own, ('col', 'rep'), axis=0, tiled=True)]
    scatter-add x20 -> x0, other arithmetic: 49.6 us -> none  [one_group(): return running.at[target].add(products * live_mask[:, None, None])]
    all_gather x2 -> x0, blocking collectives: 45 us -> none  [forward_layer(): column = lax.all_gather(own_products, 'row', axis=0, tiled=True)]
    dot_general x25 -> x0, matrix products: 32.5 us -> none  [the longest x10 13.4 us: one_group(): jnp.einsum('tji,tjh->tih', block_part, picked, preferred_element_type=jnp...]
    gather x20 -> x0, local copies, waits for them, and re-layouts: 25.2 us -> none  [the longest x10 18.7 us: one_group(): picked = source[row_part]]
  transfers between devices with their start and end apart: 7 -> 0, of which waited for: 7 -> 0; matrix products, arithmetic and copies ran while one was open for 10% -> 0% of each run, Pallas kernels for 0% -> 0%
where the time goes in v1:
time: 113 us
  Pallas kernels  102 us (90%)
  local copies, waits for them, and re-layouts  6.82 us (6%)
  other arithmetic  2.88 us (3%)
  between operations  1.4 us (1%)
    pallas_call x1, Pallas kernels, body(): pl.pallas_call(functools.partial(kernel, nx, ny, nz, slots), out_shape=[j...  102 us
    unnamed x13, local copies, waits for them, and re-layouts  6.8 us

profile of v1, /device:TPU:1, one launch (start us, length us, event | category | flops | bytes accessed | tf_op | source)
XLA Modules:
  0.0 112.6 jit_solution(6524209891799289361)
XLA Ops:
  1.3 0.7 compare_select_fusion
  2.0 0.7 compare_select_fusion.2
  2.6 0.1 convert_reduce_fusion.3
  2.8 0.1 fusion.5
  2.9 0.2 fusion.3
  3.1 0.2 convert_reduce_fusion
  3.3 0.1 convert_reduce_fusion.2
  3.4 0.1 fusion.4
  3.5 0.2 fusion.2
  3.7 0.2 convert_reduce_fusion.1
  3.9 0.1 select_reduce_fusion.1
  4.1 0.1 select_reduce_fusion
  4.3 0.0 copy-start
  4.3 1.9 %copy-done = bf16[1,1,96,128,128]{4,3,2,1,0:T(8,128)(2,1)S(1)} copy-done((bf16[1,1,96,128,128]{4,3,2,1,0:T(8,128)(2,1)S(1)}, bf16[1,1,96,128,128]{4,3,2,1,0:T(8,128)(2,1)}, u32[]{:S(2)}) %copy-start) | copy-done | bytes 3145752
  6.2 0.0 copy-start.1
  6.2 0.8 copy-done.1
  6.9 0.0 copy-start.2
  6.9 0.8 copy-done.2
  7.7 0.0 copy-start.3
  7.7 0.8 copy-done.3
  8.4 0.0 copy-start.4
  8.4 0.8 copy-done.4
  9.2 101.5 %shard_map.103 = (f32[128,128]{1,0:T(8,128)S(1)}, f32[128,128]{1,0:T(8,128)S(1)}, f32[128,128]{1,0:T(8,128)S(1)}) custom-call(s32[8,128]{1,0:T(8,128)S(1)} %fusion.6.meta, bf16[128,128]{1,0:T(8,128)(2,1)S(1)} %copy-done.1, bf16[128,128]{1,0:T(8,128)(2,1)S(1)} %copy-done.2, bf16[128,128]{1,0:T(8,128)(2,1)S(1)} %copy-done.3, bf16[128,128]{1,0:T(8,128)(2,1)S(1)} %copy-done.4, ...), custom_call_target="tpu_custom_call" | custom-call | tf_op jit(solution)/shard_map/pallas_call | solution.py:356
  110.7 0.6 copy.15
  111.3 0.6 copy.16
  112.0 0.6 copy.17
  (11 shorter events, 0.1 us)
Async XLA Ops:
  4.3 1.9 %copy-start = (bf16[1,1,96,128,128]{4,3,2,1,0:T(8,128)(2,1)S(1)}, bf16[1,1,96,128,128]{4,3,2,1,0:T(8,128)(2,1)}, u32[]{:S(2)}) copy-start(bf16[1,1,96,128,128]{4,3,2,1,0:T(8,128)(2,1)} %param.13) | copy-start | bytes 9437188
  6.2 0.8 copy-start.1
  6.9 0.8 copy-start.2
  7.7 0.8 copy-start.3
  8.4 0.8 copy-start.4

commit v2 on v0

v2 whole, which is shorter than its diff:
```python
import functools

import jax
import jax.numpy as jnp
from jax import lax
from jax.experimental import pallas as pl
from jax.experimental.pallas import tpu as pltpu
from jax.sharding import PartitionSpec as P

MESH = pl.DeviceIdType.MESH
BF = jnp.bfloat16
F32 = jnp.float32
I32 = jnp.int32
CONTRACT_LAST = (((1,), (1,)), ((), ()))
CUT = 96


def near_first(n):
    return sorted(range(1, n), key=lambda d: (min(d, n - d), d))


def far_first(n):
    return near_first(n)[::-1]


def split_dot(wide, weight):
    head = wide.astype(BF)
    rest = (wide - head.astype(F32)).astype(BF)
    return jnp.dot(head, weight, preferred_element_type=F32) + jnp.dot(rest, weight, preferred_element_type=F32)


def slot_order(group, other, count, groups):
    slots = group.shape[1]
    down = lax.broadcasted_iota(I32, (slots, slots), 0)
    along = lax.broadcasted_iota(I32, (slots, slots), 1)
    live = along < count

    def upright(row):
        return jnp.sum(jnp.where(down == along, row, 0), axis=1, keepdims=True)

    key = jnp.where(live, jnp.broadcast_to(group, (slots, slots)), groups)
    key_down = upright(key)
    other_down = upright(jnp.where(live, jnp.broadcast_to(other, (slots, slots)), 0))
    ahead = jnp.where((key == key_down) & (along < down), 1, 0)
    rank = jnp.sum(jnp.where(key < key_down, 1, ahead), axis=1, keepdims=True)
    opens = jnp.where(jnp.sum(ahead, axis=1, keepdims=True) == 0, 1, 0)
    here = rank == along

    def placed(value):
        return jnp.sum(jnp.where(here, value, 0), axis=0, keepdims=True)

    upto = jnp.sum(jnp.where(key_down <= along, 1, 0), axis=0, keepdims=True)
    found = jnp.sum(jnp.where(key_down == along, 1, 0), axis=0, keepdims=True)
    last = jnp.where(found > 0, upto - 1, slots)
    return placed(down), placed(other_down), placed(opens), last


def kernel(
    nx, ny, nz, slots,
    feat_hbm, w_in_hbm, w_hid_hbm, rows_hbm, cols_hbm, tiles_hbm, count_hbm, cot_hbm,
    logits, gw_in, gw_hid,
    w_in, w_hid, rows, cols, tiles, count, cot, meta_v, meta,
    col_src_0, col_src_1, row_src, part, send_f, rx_a, rx_b, mid_a, mid_b, ry_a, ry_b,
    send_b, r_core, mid_z, r_z, term, ar_row, ar_x, ar_y, ar_out,
    local_sem, ssem, rsem,
):
    row = lax.axis_index("row")
    col = lax.axis_index("col")
    rep = lax.axis_index("rep")
    reps_y = lax.axis_size("rep") // nx
    z, core = row // 2, row % 2
    y, x = col * reps_y + rep // nx, rep % nx
    height = cot.shape[0]
    low, high = pl.ds(0, CUT), pl.ds(CUT, height - CUT)
    col_src = (col_src_0, col_src_1)

    def device(xx, yy, zz, cc):
        return (zz * 2 + cc, yy // reps_y, (yy % reps_y) * nx + xx)

    def x_at(d):
        return (x + d) % nx, device((x + d) % nx, y, z, core)

    def y_at(d):
        return (y + d) % ny, device(x, (y + d) % ny, z, core)

    def z_at(d):
        return (z + d) % nz, device(x, y, (z + d) % nz, core)

    sibling = device(x, y, z, 1 - core)
    cross = [((z + d) % nz, device(x, y, (z + d) % nz, 1 - core)) for d in near_first(nz)]

    loads = {}
    for i, (name, src, dst) in enumerate([
        ("cot", cot_hbm, cot), ("own", feat_hbm, col_src_0.at[z, core]), ("rows", rows_hbm, rows),
        ("cols", cols_hbm, cols), ("count", count_hbm, count), ("w_in", w_in_hbm, w_in),
        ("w_hid", w_hid_hbm, w_hid), ("tiles", tiles_hbm, tiles),
    ]):
        loads[name] = pltpu.make_async_copy(src, dst, local_sem.at[i])
        loads[name].start()

    barrier = pltpu.get_barrier_semaphore()
    everyone = [x_at(d)[1] for d in near_first(nx)] + [y_at(d)[1] for d in near_first(ny)]
    everyone += [z_at(d)[1] for d in near_first(nz)] + [peer for _, peer in cross] + [sibling]
    for peer in everyone:
        pl.semaphore_signal(barrier, inc=1, device_id=peer, device_id_type=MESH)

    sends = []
    used = [0, 0]

    def new_recv(n=1):
        used[0] += n
        return used[0] - n

    def new_send(ref):
        sends.append((used[1], ref))
        used[1] += 1
        return used[1] - 1

    def push(src, dst, peer, s, r):
        pltpu.make_async_remote_copy(
            src_ref=src, dst_ref=dst, send_sem=ssem.at[s], recv_sem=rsem.at[r],
            device_id=peer, device_id_type=MESH,
        ).start()

    def landed(r, ref):
        pltpu.make_async_copy(ref, ref, rsem.at[r]).wait()

    def gather_col_start(rnd):
        buf = col_src[rnd]
        z_recv, c_recv = new_recv(nz), new_recv()
        s = new_send(buf.at[0 : nz - 1, 0])
        for d in near_first(nz):
            push(buf.at[z, core], buf.at[z, core], z_at(d)[1], s, z_recv + d)
        c_send = new_send(buf.at[:, 0])
        push(buf.at[z, core], buf.at[z, core], sibling, c_send, c_recv)
        return z_recv, c_recv, c_send

    def gather_col_pass(rnd, sems, d):
        buf = col_src[rnd]
        z_recv, c_recv, c_send = sems
        src = (z + nz - d) % nz
        landed(z_recv + d, buf.at[src, core])
        push(buf.at[src, core], buf.at[src, core], sibling, c_send, c_recv)

    def gather_col_finish(rnd, sems):
        landed(sems[1], col_src[rnd].at[:, 0])

    def gather_row_start():
        y_recv = new_recv(ny)
        s = new_send(row_src.at[0 : ny - 1, 0, low])
        for d in near_first(ny):
            push(row_src.at[y, x, low], row_src.at[y, x, low], y_at(d)[1], s, y_recv + d)
        x_recv = new_recv()
        s = new_send(row_src.at[0, 0 : nx - 1])
        for d in near_first(nx):
            push(row_src.at[y, x], row_src.at[y, x], x_at(d)[1], s, x_recv)
        return y_recv, x_recv, new_recv(), new_send(row_src.at[0 : ny - 1, 0 : nx - 1, low])

    def gather_row_high(sems):
        landed(sems[1], row_src.at[0, 0 : nx - 1])
        r = new_recv()
        s = new_send(row_src.at[0 : ny - 1, :, high])
        for d in near_first(ny):
            push(row_src.at[y, :, high], row_src.at[y, :, high], y_at(d)[1], s, r)
        return r

    def gather_row_pass(sems, d):
        y_recv, _, r, s = sems
        src = (y + ny - d) % ny
        landed(y_recv + d, row_src.at[src, x, low])
        for e in far_first(nx):
            push(row_src.at[src, x, low], row_src.at[src, x, low], x_at(e)[1], s, r)

    def gather_row_finish(sems, high_recv):
        landed(sems[2], row_src.at[0 : ny - 1, 0 : nx - 1, low])
        landed(high_recv, row_src.at[0 : ny - 1, :, high])

    unroll = 8

    def spread_forward(rnd):
        src = col_src[rnd]

        def some(turn, acc):
            for i in range(unroll):
                k = turn * unroll + i
                c = meta[1, k]
                d = jnp.dot(tiles[meta[0, k]], src[c // 2, c % 2], preferred_element_type=F32)
                acc = jnp.where(meta[2, k] > 0, d, acc + d)
                part[k] = acc.astype(BF)
            return acc

        lax.fori_loop(0, slots // unroll, some, jnp.zeros((height, height), F32))

        def place(b, _):
            send_f[rnd, b // nx, b % nx] = part[meta[3, b]]
            return 0

        lax.fori_loop(0, nx * ny, place, 0)

    def spread_backward():
        def some(turn, acc):
            for i in range(unroll):
                k = turn * unroll + i
                r = meta[5, k]
                d = jnp.dot(row_src[r // nx, r % nx], tiles[meta[4, k]], preferred_element_type=F32)
                acc = jnp.where(meta[6, k] > 0, d, acc + d)
                part[k] = acc.astype(BF)
            return acc

        lax.fori_loop(0, slots // unroll, some, jnp.zeros((height, height), F32))

        def place(b, _):
            send_b[b // 2, b % 2] = part[meta[7, b]]
            return 0

        lax.fori_loop(0, nz * 2, place, 0)

    y_turns = far_first(ny) + [0]

    def reduce_rows_start(rnd):
        buf = send_f.at[rnd]
        a_recv, b_recv = new_recv(ny), new_recv()
        a_send = new_send(rx_a.at[rnd, :, 0 : nx - 1])
        b_send = new_send(ry_b.at[rnd, 0 : ny - 1])
        for i, dy in enumerate(y_turns):
            for dx in far_first(nx):
                px, peer = x_at(dx)
                push(buf.at[(y + dy) % ny, px, low], rx_a.at[rnd, dy, x], peer, a_send, a_recv + dy)
            if i < ny - 1:
                py, peer = y_at(dy)
                push(buf.at[py, :, high], ry_b.at[rnd, y], peer, b_send, b_recv)
        ya_recv, ya_send = new_recv(), new_send(ry_a.at[rnd, 0 : ny - 1])
        return a_recv, b_recv, ya_recv, ya_send

    def reduce_rows_pass(rnd, sems, dy):
        a_recv, _, ya_recv, ya_send = sems
        landed(a_recv + dy, rx_a.at[rnd, dy, 0 : nx - 1])
        total = send_f[rnd, (y + dy) % ny, x, 0:CUT].astype(F32)
        for dx in near_first(nx):
            total += rx_a[rnd, dy, (x + dx) % nx].astype(F32)
        if dy == 0:
            mid_a[rnd, 0] = total
        else:
            mid = ry_a.at[rnd, ny + dy]
            mid[...] = total.astype(BF)
            push(mid, ry_a.at[rnd, y], y_at(dy)[1], ya_send, ya_recv)

    def reduce_rows_high(rnd, sems):
        landed(sems[1], ry_b.at[rnd, 0 : ny - 1])
        r, s = new_recv(), new_send(rx_b.at[rnd, 0 : nx - 1])
        for dx in far_first(nx) + [0]:
            px = (x + dx) % nx
            total = send_f[rnd, y, px, CUT:height].astype(F32)
            for dy in near_first(ny):
                total += ry_b[rnd, (y + dy) % ny, px].astype(F32)
            if dx == 0:
                mid_b[rnd, 0] = total
            else:
                mid = rx_b.at[rnd, nx + dx]
                mid[...] = total.astype(BF)
                push(mid, rx_b.at[rnd, x], x_at(dx)[1], s, r)
        return r

    def reduce_rows_finish(rnd, sems, high_recv):
        landed(high_recv, rx_b.at[rnd, 0 : nx - 1])
        bottom = mid_b[rnd, 0]
        for dx in near_first(nx):
            bottom += rx_b[rnd, (x + dx) % nx].astype(F32)
        landed(sems[2], ry_a.at[rnd, 0 : ny - 1])
        top = mid_a[rnd, 0]
        for dy in near_first(ny):
            top += ry_a[rnd, (y + dy) % ny].astype(F32)
        return jnp.concatenate([top, bottom], axis=0)

    def reduce_cols_start():
        r = new_recv()
        push(send_b.at[:, 1 - core], r_core, sibling, new_send(r_core), r)
        return r

    def reduce_cols_second(recv):
        landed(recv, r_core)
        r, s = new_recv(), new_send(r_z.at[0 : nz - 1])
        for d in near_first(nz):
            pz, peer = z_at(d)
            mid_z[pz] = (send_b[pz, core].astype(F32) + r_core[pz].astype(F32)).astype(BF)
            push(mid_z.at[pz], r_z.at[z], peer, s, r)
        return r

    def reduce_cols_finish(recv):
        total = send_b[z, core].astype(F32) + r_core[z].astype(F32)
        landed(recv, r_z.at[0 : nz - 1])
        for d in near_first(nz):
            total += r_z[(z + d) % nz].astype(F32)
        return total.astype(BF)

    part[slots] = jnp.zeros((height, height), BF)
    loads["cot"].wait()
    loads["own"].wait()
    row_src[y, x] = cot[...].astype(F32).T.astype(BF)
    pl.semaphore_wait(barrier, len(everyone))

    col_sems = gather_col_start(0)
    row_sems = gather_row_start()
    loads["rows"].wait()
    loads["cols"].wait()
    loads["count"].wait()
    live = count[0, 0]
    meta_v[...] = jnp.zeros_like(meta_v)
    for i, line in enumerate(slot_order(rows[0], cols[0], live, nx * ny) + slot_order(cols[0], rows[0], live, nz * 2)):
        meta_v[i : i + 1, 0:slots] = line
    meta_copy = pltpu.make_async_copy(meta_v, meta, local_sem.at[8])
    meta_copy.start()
    high_recv = gather_row_high(row_sems)
    for i in range(1, max(ny, nz)):
        if i < nz:
            gather_col_pass(0, col_sems, near_first(nz)[i - 1])
        if i < ny:
            gather_row_pass(row_sems, near_first(ny)[i - 1])
    meta_copy.wait()
    loads["tiles"].wait()
    gather_col_finish(0, col_sems)
    spread_forward(0)
    sum_sems = reduce_rows_start(0)
    for dy in y_turns[0:2]:
        reduce_rows_pass(0, sum_sems, dy)
    gather_row_finish(row_sems, high_recv)
    spread_backward()
    core_recv = reduce_cols_start()
    for dy in y_turns[2:4]:
        reduce_rows_pass(0, sum_sems, dy)
    z_recv = reduce_cols_second(core_recv)
    for dy in y_turns[4:]:
        reduce_rows_pass(0, sum_sems, dy)
    high_recv = reduce_rows_high(0, sum_sems)
    loads["w_in"].wait()
    loads["w_hid"].wait()
    mixed = reduce_rows_finish(0, sum_sems, high_recv)
    sum_first = split_dot(mixed, w_in[...])
    col_src_1[z, core] = (sum_first / (1.0 + jnp.exp(-sum_first))).astype(BF)

    col_sems = gather_col_start(1)
    mixed_t = mixed.T.astype(BF)
    sum_t = sum_first.T
    gate_t = 1.0 / (1.0 + jnp.exp(-sum_t))
    hidden_t = (sum_t * gate_t).astype(BF)
    slope_t = gate_t * (1.0 + sum_t * (1.0 - gate_t))
    grad_t = reduce_cols_finish(z_recv)
    grad_sum_t = (jnp.dot(w_hid[...], grad_t, preferred_element_type=F32) * slope_t).astype(BF)
    term[0:height] = lax.dot_general(mixed_t, grad_sum_t, CONTRACT_LAST, preferred_element_type=F32).astype(BF)
    term[height : 2 * height] = lax.dot_general(
        hidden_t, grad_t, CONTRACT_LAST, preferred_element_type=F32
    ).astype(BF)
    band = height // nz
    row_peers = [(z_at(d)[0] * 2 + core, z_at(d)[1]) for d in near_first(nz)]
    row_peers += [(pz * 2 + 1 - core, peer) for pz, peer in cross]
    row_peers += [(z * 2 + 1 - core, sibling)]

    def rows_of(i):
        return pl.ds(pl.multiple_of(i * band, band), band)

    r_row, s_row = new_recv(), new_send(ar_row.at[0 : 2 * nz - 1])
    for i, peer in row_peers:
        push(term.at[rows_of(i)], ar_row.at[row], peer, s_row, r_row)
    for d in near_first(nz):
        gather_col_pass(1, col_sems, d)
    landed(r_row, ar_row.at[0 : 2 * nz - 1])
    total = term[rows_of(row)].astype(F32)
    for i, _ in row_peers:
        total += ar_row[i].astype(F32)
    ar_x[x] = total.astype(BF)
    r_x, s_x = new_recv(), new_send(ar_x.at[0 : nx - 1])
    for d in far_first(nx):
        push(ar_x.at[x], ar_x.at[x], x_at(d)[1], s_x, r_x)
    gather_col_finish(1, col_sems)
    spread_forward(1)
    sum_sems = reduce_rows_start(1)
    landed(r_x, ar_x.at[0 : nx - 1])
    total = ar_x[0].astype(F32)
    for i in range(1, nx):
        total += ar_x[i].astype(F32)
    ar_y[y] = total.astype(BF)
    r_y, s_y = new_recv(), new_send(ar_y.at[0 : ny - 1])
    for d in far_first(ny):
        push(ar_y.at[y], ar_y.at[y], y_at(d)[1], s_y, r_y)
    for dy in y_turns[0:4]:
        reduce_rows_pass(1, sum_sems, dy)
    landed(r_y, ar_y.at[0 : ny - 1])
    total = ar_y[0].astype(F32)
    for i in range(1, ny):
        total += ar_y[i].astype(F32)
    ar_out[rows_of(row)] = total.astype(BF)
    r_out, s_out = new_recv(), new_send(ar_out.at[0 : 2 * height - band])
    for _, peer in row_peers:
        push(ar_out.at[rows_of(row)], ar_out.at[rows_of(row)], peer, s_out, r_out)
    for dy in y_turns[4:]:
        reduce_rows_pass(1, sum_sems, dy)
    high_recv = reduce_rows_high(1, sum_sems)
    landed(r_out, ar_out.at[0 : 2 * height - band])
    gw_in[...] = ar_out[0:height].astype(F32)
    gw_hid[...] = ar_out[height : 2 * height].astype(F32)
    logits[...] = split_dot(reduce_rows_finish(1, sum_sems, high_recv), w_hid[...])

    for s, ref in sends:
        pltpu.make_async_copy(ref, ref, ssem.at[s]).wait()


def write_out(a, b, c, a_out, b_out, c_out, sem):
    copies = [pltpu.make_async_copy(s, d, sem.at[i]) for i, (s, d) in enumerate([(a, a_out), (b, b_out), (c, c_out)])]
    for copy in copies:
        copy.start()
    for copy in copies:
        copy.wait()


def body(nx, features, weight_in, weight_hidden, tile_rows, tile_cols, tile_values, tile_counts, cotangent):
    nz = lax.axis_size("row") // 2
    ny = lax.axis_size(("col", "rep")) // nx
    slots, height = tile_values.shape[2], tile_values.shape[3]
    rest = height - CUT
    band = height // nz
    block = (height, height)
    vmem = pl.BlockSpec(memory_space=pltpu.VMEM)
    hbm = pl.BlockSpec(memory_space=pltpu.HBM)
    results = [jax.ShapeDtypeStruct(block, F32)] * 3
    outs = pl.pallas_call(
        functools.partial(kernel, nx, ny, nz, slots),
        out_shape=results,
        in_specs=[hbm] * 8,
        out_specs=[vmem] * 3,
        scratch_shapes=[
            pltpu.VMEM(block, BF),
            pltpu.VMEM(block, BF),
            pltpu.VMEM((1, 1, slots), I32),
            pltpu.VMEM((1, 1, slots), I32),
            pltpu.VMEM((slots,) + block, BF),
            pltpu.SMEM((1, 1), I32),
            pltpu.VMEM(block, BF),
            pltpu.VMEM((8, 128), I32),
            pltpu.SMEM((8, 128), I32),
            pltpu.VMEM((nz, 2) + block, BF),
            pltpu.VMEM((nz, 2) + block, BF),
            pltpu.VMEM((ny, nx) + block, BF),
            pltpu.VMEM((slots + 1,) + block, BF),
            pltpu.VMEM((2, ny, nx) + block, BF),
            pltpu.VMEM((2, ny, nx, CUT, height), BF),
            pltpu.VMEM((2, 2 * nx, rest, height), BF),
            pltpu.VMEM((2, 1, CUT, height), F32),
            pltpu.VMEM((2, 1, rest, height), F32),
            pltpu.VMEM((2, 2 * ny, CUT, height), BF),
            pltpu.VMEM((2, ny, nx, rest, height), BF),
            pltpu.VMEM((nz, 2) + block, BF),
            pltpu.VMEM((nz,) + block, BF),
            pltpu.VMEM((nz,) + block, BF),
            pltpu.VMEM((nz,) + block, BF),
            pltpu.VMEM((2 * height, height), BF),
            pltpu.VMEM((2 * nz, band, height), BF),
            pltpu.VMEM((nx, band, height), BF),
            pltpu.VMEM((ny, band, height), BF),
            pltpu.VMEM((2 * height, height), BF),
            pltpu.SemaphoreType.DMA((9,)),
            pltpu.SemaphoreType.DMA((40,)),
            pltpu.SemaphoreType.DMA((72,)),
        ],
        compiler_params=pltpu.CompilerParams(
            collective_id=0, has_side_effects=True, vmem_limit_bytes=56 * 1024 * 1024
        ),
    )(
        features, weight_in, weight_hidden, tile_rows, tile_cols,
        tile_values.reshape((slots,) + block), tile_counts, cotangent,
    )
    return pl.pallas_call(
        write_out,
        out_shape=results,
        in_specs=[vmem] * 3,
        out_specs=[hbm] * 3,
        scratch_shapes=[pltpu.SemaphoreType.DMA((3,))],
    )(*outs)


def solution(mesh, nx=4):
    return jax.shard_map(
        functools.partial(body, nx),
        mesh=mesh,
        in_specs=(
            P(("row", "col", "rep"), None),
            P(),
            P(),
            P("row", ("col", "rep"), None),
            P("row", ("col", "rep"), None),
            P("row", ("col", "rep"), None, None, None),
            P("row", ("col", "rep")),
            P(("row", "col", "rep"), None),
        ),
        out_specs=(P(("row", "col", "rep"), None), P(), P()),
        check_vma=False,
    )
```

time: 1060 us -> 78.6 us (0.07)
  waiting for transfers between devices: 855 us -> 0 us
  Pallas kernels: 0 us -> 77.1 us
  other arithmetic: 73.1 us -> 0 us
  blocking collectives: 45 us -> 0 us
  local copies, waits for them, and re-layouts: 34.4 us -> 0 us
  matrix products: 32.5 us -> 0 us
  between operations: 14.9 us -> 1.29 us
    reduce_scatter x4 -> x0, waiting for transfers between devices: 503 us -> none  [the longest x2 410 us: forward_layer(): lax.psum_scatter(partial_rows.astype(jnp.bfloat16), ('col', 'rep'), scatt...]
    psum x1 -> x0, waiting for transfers between devices: 271 us -> none  [body(): lax.psum((term_first, term_second), ('row', 'col', 'rep'))]
    all_gather x2 -> x0, waiting for transfers between devices: 80.7 us -> none  [backward_layer(): gathered = lax.all_gather(grad_own, ('col', 'rep'), axis=0, tiled=True)]
    pallas_call x0 -> x2, Pallas kernels: none -> 77.1 us  [the longest x1 75.5 us: body(): pl.pallas_call(functools.partial(kernel, nx, ny, nz, slots), out_shape=re...]
    scatter-add x20 -> x0, other arithmetic: 49.6 us -> none  [one_group(): return running.at[target].add(products * live_mask[:, None, None])]
    all_gather x2 -> x0, blocking collectives: 45 us -> none  [forward_layer(): column = lax.all_gather(own_products, 'row', axis=0, tiled=True)]
    dot_general x25 -> x0, matrix products: 32.5 us -> none  [the longest x10 13.4 us: one_group(): jnp.einsum('tji,tjh->tih', block_part, picked, preferred_element_type=jnp...]
    gather x20 -> x0, local copies, waits for them, and re-layouts: 25.2 us -> none  [the longest x10 18.7 us: one_group(): picked = source[row_part]]
  transfers between devices with their start and end apart: 7 -> 0, of which waited for: 7 -> 0; matrix products, arithmetic and copies ran while one was open for 10% -> 0% of each run, Pallas kernels for 0% -> 0%
where the time goes in v2:
time: 78.6 us; the launch traced here: 78.4 us
  Pallas kernels  77.1 us (98%)
  between operations  1.29 us (2%)
    pallas_call x1, Pallas kernels, body(): pl.pallas_call(functools.partial(kernel, nx, ny, nz, slots), out_shape=re...  75.5 us
    pallas_call x1, Pallas kernels, body(): pl.pallas_call(write_out, out_shape=results, in_specs=[vmem] * 3, out_spe...  1.6 us

profile of v2, /device:TPU:1, one launch (start us, length us, event | category | flops | bytes accessed | tf_op | source)
XLA Modules:
  0.0 78.4 jit_solution(16147466508702137707)
XLA Ops:
  1.3 75.5 %shard_map.103 = (f32[128,128]{1,0:T(8,128)}, f32[128,128]{1,0:T(8,128)}, f32[128,128]{1,0:T(8,128)}) custom-call(bf16[128,128]{1,0:T(8,128)(2,1)} %feat_hbm.1, bf16[128,128]{1,0:T(8,128)(2,1)} %w_in_hbm.1, bf16[128,128]{1,0:T(8,128)(2,1)} %w_hid_hbm.1, s32[1,1,96]{2,1,0:T(1,128)} %rows_hbm.1, s32[1,1,96]{2,1,0:T(1,128)} %cols_hbm.1, ...), custom_call_target="tpu_custom_call" | custom-call | tf_op jit(solution)/shard_map/pallas_call | solution.py:425
  76.8 1.6 %shard_map.104 = (f32[128,128]{1,0:T(8,128)}, f32[128,128]{1,0:T(8,128)}, f32[128,128]{1,0:T(8,128)}) custom-call(f32[128,128]{1,0:T(8,128)} %get-tuple-element.6.a, f32[128,128]{1,0:T(8,128)} %get-tuple-element.7.b, f32[128,128]{1,0:T(8,128)} %get-tuple-element.8.c), custom_call_target="tpu_custom_call" | custom-call | tf_op jit(solution)/shard_map/pallas_call | solution.py:471

commit v3 on v2

--- a/solution.py
+++ b/solution.py
@@ -175,7 +175,7 @@
         landed(sems[2], row_src.at[0 : ny - 1, 0 : nx - 1, low])
         landed(high_recv, row_src.at[0 : ny - 1, :, high])
 
-    unroll = 8
+    unroll = 32
 
     def spread_forward(rnd):
         src = col_src[rnd]
@@ -321,15 +321,13 @@
     gather_col_finish(0, col_sems)
     spread_forward(0)
     sum_sems = reduce_rows_start(0)
-    for dy in y_turns[0:2]:
-        reduce_rows_pass(0, sum_sems, dy)
     gather_row_finish(row_sems, high_recv)
     spread_backward()
     core_recv = reduce_cols_start()
-    for dy in y_turns[2:4]:
+    for dy in y_turns[0:2]:
         reduce_rows_pass(0, sum_sems, dy)
     z_recv = reduce_cols_second(core_recv)
-    for dy in y_turns[4:]:
+    for dy in y_turns[2:]:
         reduce_rows_pass(0, sum_sems, dy)
     high_recv = reduce_rows_high(0, sum_sems)
     loads["w_in"].wait()

time: 78.6 us -> 74.1 us (0.943)
  Pallas kernels: 77.1 us -> 72.6 us
    pallas_call x1, Pallas kernels: 75.5 us -> 71 us  [body(): pl.pallas_call(functools.partial(kernel, nx, ny, nz, slots), out_shape=re...]
where the time goes in v3:
time: 74.1 us; the launch traced here: 73.9 us
  Pallas kernels  72.6 us (98%)
  between operations  1.29 us (2%)
    pallas_call x1, Pallas kernels, body(): pl.pallas_call(functools.partial(kernel, nx, ny, nz, slots), out_shape=re...  71 us
    pallas_call x1, Pallas kernels, body(): pl.pallas_call(write_out, out_shape=results, in_specs=[vmem] * 3, out_spe...  1.6 us

profile of v3, /device:TPU:1, one launch (start us, length us, event | category | flops | bytes accessed | tf_op | source)
XLA Modules:
  0.0 73.9 jit_solution(4770268780199493065)
XLA Ops:
  1.3 71.0 %shard_map.103 = (f32[128,128]{1,0:T(8,128)}, f32[128,128]{1,0:T(8,128)}, f32[128,128]{1,0:T(8,128)}) custom-call(bf16[128,128]{1,0:T(8,128)(2,1)} %feat_hbm.1, bf16[128,128]{1,0:T(8,128)(2,1)} %w_in_hbm.1, bf16[128,128]{1,0:T(8,128)(2,1)} %w_hid_hbm.1, s32[1,1,96]{2,1,0:T(1,128)} %rows_hbm.1, s32[1,1,96]{2,1,0:T(1,128)} %cols_hbm.1, ...), custom_call_target="tpu_custom_call" | custom-call | tf_op jit(solution)/shard_map/pallas_call | solution.py:423
  72.3 1.6 %shard_map.104 = (f32[128,128]{1,0:T(8,128)}, f32[128,128]{1,0:T(8,128)}, f32[128,128]{1,0:T(8,128)}) custom-call(f32[128,128]{1,0:T(8,128)} %get-tuple-element.6.a, f32[128,128]{1,0:T(8,128)} %get-tuple-element.7.b, f32[128,128]{1,0:T(8,128)} %get-tuple-element.8.c), custom_call_target="tpu_custom_call" | custom-call | tf_op jit(solution)/shard_map/pallas_call | solution.py:469

commit v4 on v3

--- a/solution.py
+++ b/solution.py
@@ -61,7 +61,7 @@
     logits, gw_in, gw_hid,
     w_in, w_hid, rows, cols, tiles, count, cot, meta_v, meta,
     col_src_0, col_src_1, row_src, part, send_f, rx_a, rx_b, mid_a, mid_b, ry_a, ry_b,
-    send_b, r_core, mid_z, r_z, term, ar_row, ar_x, ar_y, ar_out,
+    send_b, r_core, mid_z, r_z, term, ar_x, ar_y, ar_core, ar_z, ar_out,
     local_sem, ssem, rsem,
 ):
     row = lax.axis_index("row")
@@ -87,7 +87,6 @@
         return (z + d) % nz, device(x, y, (z + d) % nz, core)
 
     sibling = device(x, y, z, 1 - core)
-    cross = [((z + d) % nz, device(x, y, (z + d) % nz, 1 - core)) for d in near_first(nz)]
 
     loads = {}
     for i, (name, src, dst) in enumerate([
@@ -100,7 +99,7 @@
 
     barrier = pltpu.get_barrier_semaphore()
     everyone = [x_at(d)[1] for d in near_first(nx)] + [y_at(d)[1] for d in near_first(ny)]
-    everyone += [z_at(d)[1] for d in near_first(nz)] + [peer for _, peer in cross] + [sibling]
+    everyone += [z_at(d)[1] for d in near_first(nz)] + [sibling]
     for peer in everyone:
         pl.semaphore_signal(barrier, inc=1, device_id=peer, device_id_type=MESH)
 
@@ -348,55 +347,58 @@
     term[height : 2 * height] = lax.dot_general(
         hidden_t, grad_t, CONTRACT_LAST, preferred_element_type=F32
     ).astype(BF)
-    band = height // nz
-    row_peers = [(z_at(d)[0] * 2 + core, z_at(d)[1]) for d in near_first(nz)]
-    row_peers += [(pz * 2 + 1 - core, peer) for pz, peer in cross]
-    row_peers += [(z * 2 + 1 - core, sibling)]
+    band = 2 * height // nx
 
     def rows_of(i):
         return pl.ds(pl.multiple_of(i * band, band), band)
 
-    r_row, s_row = new_recv(), new_send(ar_row.at[0 : 2 * nz - 1])
-    for i, peer in row_peers:
-        push(term.at[rows_of(i)], ar_row.at[row], peer, s_row, r_row)
-    for d in near_first(nz):
-        gather_col_pass(1, col_sems, d)
-    landed(r_row, ar_row.at[0 : 2 * nz - 1])
-    total = term[rows_of(row)].astype(F32)
-    for i, _ in row_peers:
-        total += ar_row[i].astype(F32)
-    ar_x[x] = total.astype(BF)
     r_x, s_x = new_recv(), new_send(ar_x.at[0 : nx - 1])
     for d in far_first(nx):
-        push(ar_x.at[x], ar_x.at[x], x_at(d)[1], s_x, r_x)
-    gather_col_finish(1, col_sems)
-    spread_forward(1)
-    sum_sems = reduce_rows_start(1)
+        push(term.at[rows_of(x_at(d)[0])], ar_x.at[x], x_at(d)[1], s_x, r_x)
+    for d in near_first(nz)[0:3]:
+        gather_col_pass(1, col_sems, d)
     landed(r_x, ar_x.at[0 : nx - 1])
-    total = ar_x[0].astype(F32)
-    for i in range(1, nx):
-        total += ar_x[i].astype(F32)
+    total = term[rows_of(x)].astype(F32)
+    for d in near_first(nx):
+        total += ar_x[(x + d) % nx].astype(F32)
     ar_y[y] = total.astype(BF)
     r_y, s_y = new_recv(), new_send(ar_y.at[0 : ny - 1])
     for d in far_first(ny):
         push(ar_y.at[y], ar_y.at[y], y_at(d)[1], s_y, r_y)
-    for dy in y_turns[0:4]:
-        reduce_rows_pass(1, sum_sems, dy)
+    for d in near_first(nz)[3:]:
+        gather_col_pass(1, col_sems, d)
+    gather_col_finish(1, col_sems)
+    spread_forward(1)
+    sum_sems = reduce_rows_start(1)
     landed(r_y, ar_y.at[0 : ny - 1])
     total = ar_y[0].astype(F32)
     for i in range(1, ny):
         total += ar_y[i].astype(F32)
-    ar_out[rows_of(row)] = total.astype(BF)
-    r_out, s_out = new_recv(), new_send(ar_out.at[0 : 2 * height - band])
-    for _, peer in row_peers:
-        push(ar_out.at[rows_of(row)], ar_out.at[rows_of(row)], peer, s_out, r_out)
-    for dy in y_turns[4:]:
+    ar_core[core] = total.astype(BF)
+    r_core_sum = new_recv()
+    push(ar_core.at[core], ar_core.at[core], sibling, new_send(ar_core.at[0]), r_core_sum)
+    for dy in y_turns[0:1]:
+        reduce_rows_pass(1, sum_sems, dy)
+    landed(r_core_sum, ar_core.at[0])
+    ar_z[z] = (ar_core[0].astype(F32) + ar_core[1].astype(F32)).astype(BF)
+    r_last, s_last = new_recv(), new_send(ar_z.at[0 : nz - 1])
+    for d in far_first(nz):
+        push(ar_z.at[z], ar_z.at[z], z_at(d)[1], s_last, r_last)
+    for dy in y_turns[1:]:
         reduce_rows_pass(1, sum_sems, dy)
     high_recv = reduce_rows_high(1, sum_sems)
+    landed(r_last, ar_z.at[0 : nz - 1])
+    total = ar_z[0].astype(F32)
+    for i in range(1, nz):
+        total += ar_z[i].astype(F32)
+    ar_out[rows_of(x)] = total.astype(BF)
+    r_out, s_out = new_recv(), new_send(ar_out.at[0 : 2 * height - band])
+    for d in far_first(nx):
+        push(ar_out.at[rows_of(x)], ar_out.at[rows_of(x)], x_at(d)[1], s_out, r_out)
+    logits[...] = split_dot(reduce_rows_finish(1, sum_sems, high_recv), w_hid[...])
     landed(r_out, ar_out.at[0 : 2 * height - band])
     gw_in[...] = ar_out[0:height].astype(F32)
     gw_hid[...] = ar_out[height : 2 * height].astype(F32)
-    logits[...] = split_dot(reduce_rows_finish(1, sum_sems, high_recv), w_hid[...])
 
     for s, ref in sends:
         pltpu.make_async_copy(ref, ref, ssem.at[s]).wait()
@@ -415,7 +417,7 @@
     ny = lax.axis_size(("col", "rep")) // nx
     slots, height = tile_values.shape[2], tile_values.shape[3]
     rest = height - CUT
-    band = height // nz
+    band = 2 * height // nx
     block = (height, height)
     vmem = pl.BlockSpec(memory_space=pltpu.VMEM)
     hbm = pl.BlockSpec(memory_space=pltpu.HBM)
@@ -451,9 +453,10 @@
             pltpu.VMEM((nz,) + block, BF),
             pltpu.VMEM((nz,) + block, BF),
             pltpu.VMEM((2 * height, height), BF),
-            pltpu.VMEM((2 * nz, band, height), BF),
             pltpu.VMEM((nx, band, height), BF),
             pltpu.VMEM((ny, band, height), BF),
+            pltpu.VMEM((2, band, height), BF),
+            pltpu.VMEM((nz, band, height), BF),
             pltpu.VMEM((2 * height, height), BF),
             pltpu.SemaphoreType.DMA((9,)),
             pltpu.SemaphoreType.DMA((40,)),

time: 74.1 us -> 70.3 us (0.949)
  Pallas kernels: 72.6 us -> 68.8 us
    pallas_call x1, Pallas kernels: 71 us -> 67.2 us  [body(): pl.pallas_call(functools.partial(kernel, nx, ny, nz, slots), out_shape=re...]
where the time goes in v4:
time: 70.3 us; the launch traced here: 70.1 us
  Pallas kernels  68.8 us (98%)
  between operations  1.29 us (2%)
    pallas_call x1, Pallas kernels, body(): pl.pallas_call(functools.partial(kernel, nx, ny, nz, slots), out_shape=re...  67.2 us
    pallas_call x1, Pallas kernels, body(): pl.pallas_call(write_out, out_shape=results, in_specs=[vmem] * 3, out_spe...  1.6 us

profile of v4, /device:TPU:1, one launch (start us, length us, event | category | flops | bytes accessed | tf_op | source)
XLA Modules:
  0.0 70.1 jit_solution(5436075235672202158)
XLA Ops:
  1.3 67.2 %shard_map.103 = (f32[128,128]{1,0:T(8,128)}, f32[128,128]{1,0:T(8,128)}, f32[128,128]{1,0:T(8,128)}) custom-call(bf16[128,128]{1,0:T(8,128)(2,1)} %feat_hbm.1, bf16[128,128]{1,0:T(8,128)(2,1)} %w_in_hbm.1, bf16[128,128]{1,0:T(8,128)(2,1)} %w_hid_hbm.1, s32[1,1,96]{2,1,0:T(1,128)} %rows_hbm.1, s32[1,1,96]{2,1,0:T(1,128)} %cols_hbm.1, ...), custom_call_target="tpu_custom_call" | custom-call | tf_op jit(solution)/shard_map/pallas_call | solution.py:425
  68.5 1.6 %shard_map.104 = (f32[128,128]{1,0:T(8,128)}, f32[128,128]{1,0:T(8,128)}, f32[128,128]{1,0:T(8,128)}) custom-call(f32[128,128]{1,0:T(8,128)} %get-tuple-element.6.a, f32[128,128]{1,0:T(8,128)} %get-tuple-element.7.b, f32[128,128]{1,0:T(8,128)} %get-tuple-element.8.c), custom_call_target="tpu_custom_call" | custom-call | tf_op jit(solution)/shard_map/pallas_call | solution.py:472

commit v5 on v4

--- a/solution.py
+++ b/solution.py
@@ -71,7 +71,10 @@
     z, core = row // 2, row % 2
     y, x = col * reps_y + rep // nx, rep % nx
     height = cot.shape[0]
-    low, high = pl.ds(0, CUT), pl.ds(CUT, height - CUT)
+    rest = height - CUT
+    high, low = pl.ds(0, rest), pl.ds(rest, CUT)
+    pieces = (((0, CUT // 2), (CUT // 2, CUT // 2)), ((0, CUT),))
+    early = rest + CUT // 2
     col_src = (col_src_0, col_src_1)
 
     def device(xx, yy, zz, cc):
@@ -124,21 +127,25 @@
     def landed(r, ref):
         pltpu.make_async_copy(ref, ref, rsem.at[r]).wait()
 
-    def gather_col_start(rnd):
+    def gather_col_start(rnd, *cuts):
         buf = col_src[rnd]
-        z_recv, c_recv = new_recv(nz), new_recv()
-        s = new_send(buf.at[0 : nz - 1, 0])
+        runs = [(pl.ds(*cut), new_recv(nz), new_send(buf.at[0 : nz - 1, 0, pl.ds(*cut)])) for cut in cuts]
+        return runs, new_recv(), new_send(buf.at[:, 0])
+
+    def gather_col_run(rnd, sems, i):
+        buf = col_src[rnd]
+        runs, c_recv, c_send = sems
+        some, z_recv, s = runs[i]
         for d in near_first(nz):
-            push(buf.at[z, core], buf.at[z, core], z_at(d)[1], s, z_recv + d)
-        c_send = new_send(buf.at[:, 0])
-        push(buf.at[z, core], buf.at[z, core], sibling, c_send, c_recv)
-        return z_recv, c_recv, c_send
+            push(buf.at[z, core, some], buf.at[z, core, some], z_at(d)[1], s, z_recv + d)
+        push(buf.at[z, core, some], buf.at[z, core, some], sibling, c_send, c_recv)
 
     def gather_col_pass(rnd, sems, d):
         buf = col_src[rnd]
-        z_recv, c_recv, c_send = sems
+        runs, c_recv, c_send = sems
         src = (z + nz - d) % nz
-        landed(z_recv + d, buf.at[src, core])
+        for some, z_recv, _ in runs:
+            landed(z_recv + d, buf.at[src, core, some])
         push(buf.at[src, core], buf.at[src, core], sibling, c_send, c_recv)
 
     def gather_col_finish(rnd, sems):
@@ -218,38 +225,44 @@
 
     def reduce_rows_start(rnd):
         buf = send_f.at[rnd]
-        a_recv, b_recv = new_recv(ny), new_recv()
-        a_send = new_send(rx_a.at[rnd, :, 0 : nx - 1])
-        b_send = new_send(ry_b.at[rnd, 0 : ny - 1])
-        for i, dy in enumerate(y_turns):
-            for dx in far_first(nx):
-                px, peer = x_at(dx)
-                push(buf.at[(y + dy) % ny, px, low], rx_a.at[rnd, dy, x], peer, a_send, a_recv + dy)
-            if i < ny - 1:
-                py, peer = y_at(dy)
-                push(buf.at[py, :, high], ry_b.at[rnd, y], peer, b_send, b_recv)
-        ya_recv, ya_send = new_recv(), new_send(ry_a.at[rnd, 0 : ny - 1])
-        return a_recv, b_recv, ya_recv, ya_send
-
-    def reduce_rows_pass(rnd, sems, dy):
-        a_recv, _, ya_recv, ya_send = sems
-        landed(a_recv + dy, rx_a.at[rnd, dy, 0 : nx - 1])
-        total = send_f[rnd, (y + dy) % ny, x, 0:CUT].astype(F32)
+        b_recv, b_send = new_recv(), new_send(ry_b.at[rnd, 0 : ny - 1])
+        sems = []
+        for j, (first, count) in enumerate(pieces[rnd]):
+            a_recv, a_send = new_recv(ny), new_send(rx_a.at[rnd, :, 0 : nx - 1, pl.ds(first, count)])
+            for i, dy in enumerate(y_turns):
+                for dx in far_first(nx):
+                    px, peer = x_at(dx)
+                    push(
+                        buf.at[(y + dy) % ny, px, pl.ds(rest + first, count)],
+                        rx_a.at[rnd, dy, x, pl.ds(first, count)], peer, a_send, a_recv + dy,
+                    )
+                if i < ny - 1 and j == 0:
+                    py, peer = y_at(dy)
+                    push(buf.at[py, :, high], ry_b.at[rnd, y], peer, b_send, b_recv)
+            sems.append((a_recv, new_recv(), new_send(ry_a.at[rnd, 0 : ny - 1, pl.ds(first, count)])))
+        return sems, b_recv
+
+    def reduce_rows_pass(rnd, sems, dy, j=0):
+        a_recv, ya_recv, ya_send = sems[0][j]
+        first, count = pieces[rnd][j]
+        some = pl.ds(first, count)
+        landed(a_recv + dy, rx_a.at[rnd, dy, 0 : nx - 1, some])
+        total = send_f[rnd, (y + dy) % ny, x, pl.ds(rest + first, count)].astype(F32)
         for dx in near_first(nx):
-            total += rx_a[rnd, dy, (x + dx) % nx].astype(F32)
+            total += rx_a[rnd, dy, (x + dx) % nx, some].astype(F32)
         if dy == 0:
-            mid_a[rnd, 0] = total
+            mid_a[rnd, 0, some] = total
         else:
-            mid = ry_a.at[rnd, ny + dy]
+            mid = ry_a.at[rnd, ny + dy, some]
             mid[...] = total.astype(BF)
-            push(mid, ry_a.at[rnd, y], y_at(dy)[1], ya_send, ya_recv)
+            push(mid, ry_a.at[rnd, y, some], y_at(dy)[1], ya_send, ya_recv)
 
     def reduce_rows_high(rnd, sems):
         landed(sems[1], ry_b.at[rnd, 0 : ny - 1])
         r, s = new_recv(), new_send(rx_b.at[rnd, 0 : nx - 1])
         for dx in far_first(nx) + [0]:
             px = (x + dx) % nx
-            total = send_f[rnd, y, px, CUT:height].astype(F32)
+            total = send_f[rnd, y, px, 0:rest].astype(F32)
             for dy in near_first(ny):
                 total += ry_b[rnd, (y + dy) % ny, px].astype(F32)
             if dx == 0:
@@ -260,16 +273,21 @@
                 push(mid, rx_b.at[rnd, x], x_at(dx)[1], s, r)
         return r
 
-    def reduce_rows_finish(rnd, sems, high_recv):
+    def reduce_rows_finish_high(rnd, high_recv):
         landed(high_recv, rx_b.at[rnd, 0 : nx - 1])
-        bottom = mid_b[rnd, 0]
+        total = mid_b[rnd, 0]
         for dx in near_first(nx):
-            bottom += rx_b[rnd, (x + dx) % nx].astype(F32)
-        landed(sems[2], ry_a.at[rnd, 0 : ny - 1])
-        top = mid_a[rnd, 0]
+            total += rx_b[rnd, (x + dx) % nx].astype(F32)
+        return total
+
+    def reduce_rows_finish_low(rnd, sems, j=0):
+        first, count = pieces[rnd][j]
+        some = pl.ds(first, count)
+        landed(sems[0][j][1], ry_a.at[rnd, 0 : ny - 1, some])
+        total = mid_a[rnd, 0, some]
         for dy in near_first(ny):
-            top += ry_a[rnd, (y + dy) % ny].astype(F32)
-        return jnp.concatenate([top, bottom], axis=0)
+            total += ry_a[rnd, (y + dy) % ny, some].astype(F32)
+        return total
 
     def reduce_cols_start():
         r = new_recv()
@@ -298,7 +316,8 @@
     row_src[y, x] = cot[...].astype(F32).T.astype(BF)
     pl.semaphore_wait(barrier, len(everyone))
 
-    col_sems = gather_col_start(0)
+    col_sems = gather_col_start(0, (0, height))
+    gather_col_run(0, col_sems, 0)
     row_sems = gather_row_start()
     loads["rows"].wait()
     loads["cols"].wait()
@@ -328,14 +347,34 @@
     z_recv = reduce_cols_second(core_recv)
     for dy in y_turns[2:]:
         reduce_rows_pass(0, sum_sems, dy)
+    for dy in y_turns[:2]:
+        reduce_rows_pass(0, sum_sems, dy, 1)
     high_recv = reduce_rows_high(0, sum_sems)
+    for dy in y_turns[2:7]:
+        reduce_rows_pass(0, sum_sems, dy, 1)
     loads["w_in"].wait()
     loads["w_hid"].wait()
-    mixed = reduce_rows_finish(0, sum_sems, high_recv)
-    sum_first = split_dot(mixed, w_in[...])
-    col_src_1[z, core] = (sum_first / (1.0 + jnp.exp(-sum_first))).astype(BF)
-
-    col_sems = gather_col_start(1)
+
+    col_sems = gather_col_start(1, (0, early), (early, height - early))
+
+    def activate(mixed):
+        sums = split_dot(mixed, w_in[...])
+        return sums, (sums / (1.0 + jnp.exp(-sums))).astype(BF)
+
+    mixed_high = reduce_rows_finish_high(0, high_recv)
+    mixed_early = jnp.concatenate([mixed_high, reduce_rows_finish_low(0, sum_sems, 0)], axis=0)
+    sum_early, hidden_early = activate(mixed_early)
+    col_src_1[z, core, 0:early] = hidden_early
+    gather_col_run(1, col_sems, 0)
+    for dy in y_turns[7:]:
+        reduce_rows_pass(0, sum_sems, dy, 1)
+    mixed_late = reduce_rows_finish_low(0, sum_sems, 1)
+    sum_late, hidden_late = activate(mixed_late)
+    col_src_1[z, core, early:height] = hidden_late
+    gather_col_run(1, col_sems, 1)
+    mixed = jnp.concatenate([mixed_early, mixed_late], axis=0)
+    sum_first = jnp.concatenate([sum_early, sum_late], axis=0)
+
     mixed_t = mixed.T.astype(BF)
     sum_t = sum_first.T
     gate_t = 1.0 / (1.0 + jnp.exp(-sum_t))
@@ -384,9 +423,11 @@
     r_last, s_last = new_recv(), new_send(ar_z.at[0 : nz - 1])
     for d in far_first(nz):
         push(ar_z.at[z], ar_z.at[z], z_at(d)[1], s_last, r_last)
-    for dy in y_turns[1:]:
+    for dy in y_turns[1:-2]:
         reduce_rows_pass(1, sum_sems, dy)
     high_recv = reduce_rows_high(1, sum_sems)
+    for dy in y_turns[-2:]:
+        reduce_rows_pass(1, sum_sems, dy)
     landed(r_last, ar_z.at[0 : nz - 1])
     total = ar_z[0].astype(F32)
     for i in range(1, nz):
@@ -395,7 +436,8 @@
     r_out, s_out = new_recv(), new_send(ar_out.at[0 : 2 * height - band])
     for d in far_first(nx):
         push(ar_out.at[rows_of(x)], ar_out.at[rows_of(x)], x_at(d)[1], s_out, r_out)
-    logits[...] = split_dot(reduce_rows_finish(1, sum_sems, high_recv), w_hid[...])
+    mixed = jnp.concatenate([reduce_rows_finish_high(1, high_recv), reduce_rows_finish_low(1, sum_sems)], axis=0)
+    logits[...] = split_dot(mixed, w_hid[...])
     landed(r_out, ar_out.at[0 : 2 * height - band])
     gw_in[...] = ar_out[0:height].astype(F32)
     gw_hid[...] = ar_out[height : 2 * height].astype(F32)
@@ -459,8 +501,8 @@
             pltpu.VMEM((nz, band, height), BF),
             pltpu.VMEM((2 * height, height), BF),
             pltpu.SemaphoreType.DMA((9,)),
-            pltpu.SemaphoreType.DMA((40,)),
-            pltpu.SemaphoreType.DMA((72,)),
+            pltpu.SemaphoreType.DMA((48,)),
+            pltpu.SemaphoreType.DMA((88,)),
         ],
         compiler_params=pltpu.CompilerParams(
             collective_id=0, has_side_effects=True, vmem_limit_bytes=56 * 1024 * 1024

time: 70.3 us -> 68.9 us (0.980)
  Pallas kernels: 68.8 us -> 67.4 us
    pallas_call x1, Pallas kernels: 67.2 us -> 65.8 us  [body(): pl.pallas_call(functools.partial(kernel, nx, ny, nz, slots), out_shape=re...]
where the time goes in v5:
time: 68.9 us; the launch traced here: 68.7 us
  Pallas kernels  67.4 us (98%)
  between operations  1.29 us (2%)
    pallas_call x1, Pallas kernels, body(): pl.pallas_call(functools.partial(kernel, nx, ny, nz, slots), out_shape=re...  65.8 us
    pallas_call x1, Pallas kernels, body(): pl.pallas_call(write_out, out_shape=results, in_specs=[vmem] * 3, out_spe...  1.6 us

profile of v5, /device:TPU:1, one launch (start us, length us, event | category | flops | bytes accessed | tf_op | source)
XLA Modules:
  0.0 68.7 jit_solution(3159986167167614312)
XLA Ops:
  1.3 65.8 %shard_map.103 = (f32[128,128]{1,0:T(8,128)}, f32[128,128]{1,0:T(8,128)}, f32[128,128]{1,0:T(8,128)}) custom-call(bf16[128,128]{1,0:T(8,128)(2,1)} %feat_hbm.1, bf16[128,128]{1,0:T(8,128)(2,1)} %w_in_hbm.1, bf16[128,128]{1,0:T(8,128)(2,1)} %w_hid_hbm.1, s32[1,1,96]{2,1,0:T(1,128)} %rows_hbm.1, s32[1,1,96]{2,1,0:T(1,128)} %cols_hbm.1, ...), custom_call_target="tpu_custom_call" | custom-call | tf_op jit(solution)/shard_map/pallas_call | solution.py:467
  67.1 1.6 %shard_map.104 = (f32[128,128]{1,0:T(8,128)}, f32[128,128]{1,0:T(8,128)}, f32[128,128]{1,0:T(8,128)}) custom-call(f32[128,128]{1,0:T(8,128)} %get-tuple-element.6.a, f32[128,128]{1,0:T(8,128)} %get-tuple-element.7.b, f32[128,128]{1,0:T(8,128)} %get-tuple-element.8.c), custom_call_target="tpu_custom_call" | custom-call | tf_op jit(solution)/shard_map/pallas_call | solution.py:514

commit v6 on v5

--- a/solution.py
+++ b/solution.py
@@ -43,7 +43,7 @@
     other_down = upright(jnp.where(live, jnp.broadcast_to(other, (slots, slots)), 0))
     ahead = jnp.where((key == key_down) & (along < down), 1, 0)
     rank = jnp.sum(jnp.where(key < key_down, 1, ahead), axis=1, keepdims=True)
-    opens = jnp.where(jnp.sum(ahead, axis=1, keepdims=True) == 0, 1, 0)
+    follows = jnp.where(jnp.sum(ahead, axis=1, keepdims=True) == 0, 0, 1)
     here = rank == along
 
     def placed(value):
@@ -52,7 +52,7 @@
     upto = jnp.sum(jnp.where(key_down <= along, 1, 0), axis=0, keepdims=True)
     found = jnp.sum(jnp.where(key_down == along, 1, 0), axis=0, keepdims=True)
     last = jnp.where(found > 0, upto - 1, slots)
-    return placed(down), placed(other_down), placed(opens), last
+    return placed(down), placed(other_down), placed(follows), last
 
 
 def kernel(
@@ -191,7 +191,7 @@
                 k = turn * unroll + i
                 c = meta[1, k]
                 d = jnp.dot(tiles[meta[0, k]], src[c // 2, c % 2], preferred_element_type=F32)
-                acc = jnp.where(meta[2, k] > 0, d, acc + d)
+                acc = acc * meta[2, k].astype(F32) + d
                 part[k] = acc.astype(BF)
             return acc
 
@@ -201,7 +201,7 @@
             send_f[rnd, b // nx, b % nx] = part[meta[3, b]]
             return 0
 
-        lax.fori_loop(0, nx * ny, place, 0)
+        lax.fori_loop(0, nx * ny, place, 0, unroll=8)
 
     def spread_backward():
         def some(turn, acc):
@@ -209,7 +209,7 @@
                 k = turn * unroll + i
                 r = meta[5, k]
                 d = jnp.dot(row_src[r // nx, r % nx], tiles[meta[4, k]], preferred_element_type=F32)
-                acc = jnp.where(meta[6, k] > 0, d, acc + d)
+                acc = acc * meta[6, k].astype(F32) + d
                 part[k] = acc.astype(BF)
             return acc
 
@@ -219,7 +219,7 @@
             send_b[b // 2, b % 2] = part[meta[7, b]]
             return 0
 
-        lax.fori_loop(0, nz * 2, place, 0)
+        lax.fori_loop(0, nz * 2, place, 0, unroll=8)
 
     y_turns = far_first(ny) + [0]
 

time: 68.9 us -> 68.5 us (level)
  no operation moved by 1% of the time
where the time goes in v6:
time: 68.5 us; the launch traced here: 68.3 us
  Pallas kernels  67 us (98%)
  between operations  1.29 us (2%)
    pallas_call x1, Pallas kernels, body(): pl.pallas_call(functools.partial(kernel, nx, ny, nz, slots), out_shape=re...  65.4 us
    pallas_call x1, Pallas kernels, body(): pl.pallas_call(write_out, out_shape=results, in_specs=[vmem] * 3, out_spe...  1.6 us

profile of v6, /device:TPU:1, one launch (start us, length us, event | category | flops | bytes accessed | tf_op | source)
XLA Modules:
  0.0 68.3 jit_solution(8936582733505922337)
XLA Ops:
  1.3 65.4 %shard_map.103 = (f32[128,128]{1,0:T(8,128)}, f32[128,128]{1,0:T(8,128)}, f32[128,128]{1,0:T(8,128)}) custom-call(bf16[128,128]{1,0:T(8,128)(2,1)} %feat_hbm.1, bf16[128,128]{1,0:T(8,128)(2,1)} %w_in_hbm.1, bf16[128,128]{1,0:T(8,128)(2,1)} %w_hid_hbm.1, s32[1,1,96]{2,1,0:T(1,128)} %rows_hbm.1, s32[1,1,96]{2,1,0:T(1,128)} %cols_hbm.1, ...), custom_call_target="tpu_custom_call" | custom-call | tf_op jit(solution)/shard_map/pallas_call | solution.py:467
  66.7 1.6 %shard_map.104 = (f32[128,128]{1,0:T(8,128)}, f32[128,128]{1,0:T(8,128)}, f32[128,128]{1,0:T(8,128)}) custom-call(f32[128,128]{1,0:T(8,128)} %get-tuple-element.6.a, f32[128,128]{1,0:T(8,128)} %get-tuple-element.7.b, f32[128,128]{1,0:T(8,128)} %get-tuple-element.8.c), custom_call_target="tpu_custom_call" | custom-call | tf_op jit(solution)/shard_map/pallas_call | solution.py:514

commit v7 on v6

--- a/solution.py
+++ b/solution.py
@@ -126,6 +126,13 @@
 
     def landed(r, ref):
         pltpu.make_async_copy(ref, ref, rsem.at[r]).wait()
+
+    drained = [0]
+
+    def drain(upto):
+        for s, ref in sends[drained[0] : upto]:
+            pltpu.make_async_copy(ref, ref, ssem.at[s]).wait()
+        drained[0] = upto
 
     def gather_col_start(rnd, *cuts):
         buf = col_src[rnd]
@@ -408,6 +415,7 @@
         gather_col_pass(1, col_sems, d)
     gather_col_finish(1, col_sems)
     spread_forward(1)
+    before = len(sends)
     sum_sems = reduce_rows_start(1)
     landed(r_y, ar_y.at[0 : ny - 1])
     total = ar_y[0].astype(F32)
@@ -436,14 +444,14 @@
     r_out, s_out = new_recv(), new_send(ar_out.at[0 : 2 * height - band])
     for d in far_first(nx):
         push(ar_out.at[rows_of(x)], ar_out.at[rows_of(x)], x_at(d)[1], s_out, r_out)
+    drain(before)
     mixed = jnp.concatenate([reduce_rows_finish_high(1, high_recv), reduce_rows_finish_low(1, sum_sems)], axis=0)
     logits[...] = split_dot(mixed, w_hid[...])
     landed(r_out, ar_out.at[0 : 2 * height - band])
     gw_in[...] = ar_out[0:height].astype(F32)
     gw_hid[...] = ar_out[height : 2 * height].astype(F32)
 
-    for s, ref in sends:
-        pltpu.make_async_copy(ref, ref, ssem.at[s]).wait()
+    drain(len(sends))
 
 
 def write_out(a, b, c, a_out, b_out, c_out, sem):

time: 68.5 us -> 68.5 us (level)
  no operation moved by 1% of the time
where the time goes in v7:
time: 68.5 us; the launch traced here: 68.3 us
  Pallas kernels  67 us (98%)
  between operations  1.29 us (2%)
    pallas_call x1, Pallas kernels, body(): pl.pallas_call(functools.partial(kernel, nx, ny, nz, slots), out_shape=re...  65.4 us
    pallas_call x1, Pallas kernels, body(): pl.pallas_call(write_out, out_shape=results, in_specs=[vmem] * 3, out_spe...  1.6 us

profile of v7, /device:TPU:1, one launch (start us, length us, event | category | flops | bytes accessed | tf_op | source)
XLA Modules:
  0.0 68.3 jit_solution(10376624104971054538)
XLA Ops:
  1.3 65.4 %shard_map.103 = (f32[128,128]{1,0:T(8,128)}, f32[128,128]{1,0:T(8,128)}, f32[128,128]{1,0:T(8,128)}) custom-call(bf16[128,128]{1,0:T(8,128)(2,1)} %feat_hbm.1, bf16[128,128]{1,0:T(8,128)(2,1)} %w_in_hbm.1, bf16[128,128]{1,0:T(8,128)(2,1)} %w_hid_hbm.1, s32[1,1,96]{2,1,0:T(1,128)} %rows_hbm.1, s32[1,1,96]{2,1,0:T(1,128)} %cols_hbm.1, ...), custom_call_target="tpu_custom_call" | custom-call | tf_op jit(solution)/shard_map/pallas_call | solution.py:475
  66.7 1.6 %shard_map.104 = (f32[128,128]{1,0:T(8,128)}, f32[128,128]{1,0:T(8,128)}, f32[128,128]{1,0:T(8,128)}) custom-call(f32[128,128]{1,0:T(8,128)} %get-tuple-element.6.a, f32[128,128]{1,0:T(8,128)} %get-tuple-element.7.b, f32[128,128]{1,0:T(8,128)} %get-tuple-element.8.c), custom_call_target="tpu_custom_call" | custom-call | tf_op jit(solution)/shard_map/pallas_call | solution.py:522
